TPU v7x, 256 devices: a whole 4x4x8 slice. The times are simulated.
256 devices in a mesh: flow: 16 (over y, x), cy: 8 (over z_hi, core), cz: 2 (over z_lo).
Axes of the slice: x: 4, y: 4, z: 8 (z_hi: 4, z_lo: 2; z = z_hi * 2 + z_lo), core: 2. Of those that a mesh axis runs over, the one named last changes fastest.
Arguments:
- flow_pops: float32 [19, 256, 128, 256], P(None, 'flow', 'cy', 'cz'), may hold values from 0.02 to 0.22
- ion_pos: float32 [7, 256, 128, 256], P(None, 'flow', 'cy', 'cz'), may hold values from 0.05 to 0.25
- ion_neg: float32 [7, 256, 128, 256], P(None, 'flow', 'cy', 'cz'), may hold values from 0.05 to 0.25
- gray_class: int32 [256, 128, 256], P('flow', 'cy', 'cz'), may hold values from 0 to 15
- fraction_table: float32 [16], replicated, may hold values from 0 to 0.9
Outputs:
- flow_new: float32 [19, 256, 128, 256], P(None, 'flow', 'cy', 'cz')
- pos_new: float32 [7, 256, 128, 256], P(None, 'flow', 'cy', 'cz')
- neg_new: float32 [7, 256, 128, 256], P(None, 'flow', 'cy', 'cz')
- potential: float32 [256, 128, 256], P('flow', 'cy', 'cz')
All inputs are finite; a program needn't handle non-finite values.
Results may differ from a plain program's by a relative error of at most 0.0003.
Values sent between devices are 32-bit elements; how exact they have to be, the bound alone decides.
A program may use at most 192 MiB of HBM per device.

v0:
```python
import functools
import math

import jax
import jax.numpy as jnp
import numpy as np
from jax import lax
from jax.experimental import pallas as pl
from jax.experimental.pallas import tpu as pltpu
from jax.sharding import PartitionSpec as P

flow_dirs = (
    (0, 0, 0),
    (1, 0, 0),
    (-1, 0, 0),
    (0, 1, 0),
    (0, -1, 0),
    (0, 0, 1),
    (0, 0, -1),
    (1, 1, 0),
    (-1, -1, 0),
    (1, -1, 0),
    (-1, 1, 0),
    (1, 0, 1),
    (-1, 0, -1),
    (1, 0, -1),
    (-1, 0, 1),
    (0, 1, 1),
    (0, -1, -1),
    (0, 1, -1),
    (0, -1, 1),
)
flow_weights = (1.0 / 3.0,) + (1.0 / 18.0,) * 6 + (1.0 / 36.0,) * 12
ion_weights = (0.25,) + (0.125,) * 6
tau_flow = 0.8
tau_ion = 0.9
coupling = 2.0
mobility = 0.5
NX, NY, NZ = 256, 128, 256
FLOW, CY, CZ = 16, 8, 2
MESH = pl.DeviceIdType.MESH
f32 = jnp.float32

DIRS = flow_dirs + flow_dirs[:7] + flow_dirs[:7]
FACE = {
    (axis, sign): [q for q in range(33) if DIRS[q][axis] == sign]
    for axis in range(3)
    for sign in (1, -1)
}


def cas_table(points_k, points_n, length):
    product = (points_k[:, None].astype(np.int64) * points_n[None, :]) % length
    angle = product * (2.0 * math.pi / length)
    return (np.cos(angle) + np.sin(angle)).astype(np.float32)


def tables():
    order = np.array([16 * a + b for b in range(16) for a in range(16)])
    hx = cas_table(order, order, NX)
    hy = cas_table(np.arange(NY), np.arange(NY), NY)
    hz = cas_table(np.arange(NZ), np.arange(NZ), NZ)

    def lam(modes, length):
        return 4.0 * np.sin(np.pi * modes / length) ** 2

    rows = np.zeros((NX + NY + 8, 128))
    rows[:NX] = lam(order, NX)[:, None]
    rows[NX : NX + NY] = lam(np.arange(NY), NY)[:, None]
    rows[NX + NY : NX + NY + 2] = lam(np.arange(NZ), NZ).reshape(2, 128)
    return hx, hy, hz, rows.astype(np.float32)


def place():
    return lax.axis_index("flow"), lax.axis_index("cy"), lax.axis_index("cz")


def fdot(left, right):
    return jnp.dot(left, right, precision=lax.Precision.HIGHEST, preferred_element_type=f32)


def settle(ref, sem):
    pltpu.make_async_copy(ref, ref, sem).wait()


def column_mask(shape, index):
    return lax.broadcasted_iota(jnp.int32, shape, 1) == index


def row_mask(shape, index):
    return lax.broadcasted_iota(jnp.int32, shape, 0) == index


def swap_across_plane(source, target, send_sem, recv_sem):
    _, cy, cz = place()
    me = cz * CY + cy

    def step(k, carry):
        other = lax.rem(me + k, 16)
        pltpu.make_async_remote_copy(
            src_ref=source(other),
            dst_ref=target(me),
            send_sem=send_sem,
            recv_sem=recv_sem,
            device_id={"cy": lax.rem(other, CY), "cz": lax.div(other, CY)},
            device_id_type=MESH,
        ).start()
        return carry

    lax.fori_loop(1, 16, step, 0)
    pltpu.make_async_copy(source(me), target(me), recv_sem).start()


def swap_along_flow(source, target, send_sem, recv_sem):
    me, _, _ = place()

    def step(k, carry):
        other = lax.rem(me + k, 16)
        pltpu.make_async_remote_copy(
            src_ref=source(other),
            dst_ref=target(me),
            send_sem=send_sem,
            recv_sem=recv_sem,
            device_id={"flow": other},
            device_id_type=MESH,
        ).start()
        return carry

    lax.fori_loop(1, 16, step, 0)
    pltpu.make_async_copy(source(me), target(me), recv_sem).start()


def rows_at(ref, start, count):
    return ref.at[pl.ds(pl.multiple_of(start, count), count), :]


def halves_at(ref, start, count):
    return ref.at[:, pl.ds(pl.multiple_of(start, count), count), :]


def potential_kernel(
    pos_ref,
    neg_ref,
    hx_ref,
    hy_ref,
    hz_ref,
    lam_ref,
    charge_out,
    phi_out,
    xh_out,
    yh_out,
    zh_out,
    ions,
    s0,
    r0,
    s1,
    r1,
    s2,
    r2,
    s3,
    r3,
    s4,
    r4,
    s5,
    r5,
    ys,
    zs,
    xh,
    yh,
    zh,
    load_sem,
    send_sem,
    recv_sem,
    hsend_sem,
    hrecv_sem,
):
    flow, cy, cz = place()
    load_pos = pltpu.make_async_copy(pos_ref, ions.at[pl.ds(0, 7)], load_sem.at[0])
    load_neg = pltpu.make_async_copy(neg_ref, ions.at[pl.ds(7, 7)], load_sem.at[1])
    load_pos.start()
    load_neg.start()
    barrier = pltpu.get_barrier_semaphore()
    me = cz * CY + cy

    def greet(k, carry):
        other = lax.rem(me + k, 16)
        pl.semaphore_signal(
            barrier,
            inc=1,
            device_id={"cy": lax.rem(other, CY), "cz": lax.div(other, CY)},
            device_id_type=MESH,
        )
        pl.semaphore_signal(
            barrier, inc=1, device_id={"flow": lax.rem(flow + k, 16)}, device_id_type=MESH
        )
        return carry

    lax.fori_loop(1, 16, greet, 0)
    load_pos.wait()
    load_neg.wait()
    pos = ions[0]
    neg = ions[7]
    for q in range(1, 7):
        pos = pos + ions[q]
        neg = neg + ions[7 + q]
    s0[...] = pos - neg
    pl.semaphore_wait(barrier, 30)

    swap_across_plane(
        lambda b: rows_at(s0, 16 * b, 16),
        lambda b: rows_at(r0, 16 * b, 16),
        send_sem.at[0],
        recv_sem.at[0],
    )
    charge_out[...] = s0[...]
    settle(r0, recv_sem.at[0])
    hy = hy_ref[...]
    half = [fdot(hy, r0[128 * c : 128 * c + 128, :]) for c in range(2)]
    spectrum = fdot(jnp.concatenate(half, axis=1), hz_ref[...])
    s1[0] = spectrum[:, :128]
    s1[1] = spectrum[:, 128:]
    swap_along_flow(
        lambda a: halves_at(s1, 8 * a, 8),
        lambda a: halves_at(r1, 8 * a, 8),
        send_sem.at[1],
        recv_sem.at[1],
    )
    settle(r1, recv_sem.at[1])
    for b in range(16):
        s2[16 * b : 16 * b + 16, :] = r1[b // CY, pl.ds(b % CY, 16, stride=8), :]
    swap_across_plane(
        lambda b: rows_at(s2, 16 * b, 16),
        lambda b: rows_at(r2, 16 * b, 16),
        send_sem.at[2],
        recv_sem.at[2],
    )
    total = (
        lam_ref[0:NX, :]
        + lam_ref[pl.ds(NX + CY * flow + cy, 1), :]
        + lam_ref[pl.ds(NX + NY + cz, 1), :]
    )
    scale = coupling / (NX * NY * NZ)
    green = jnp.where(total > 0.0, scale / jnp.where(total > 0.0, total, 1.0), 0.0)
    settle(r2, recv_sem.at[2])
    modes = green * fdot(hx_ref[...], r2[...])
    s3[...] = fdot(hx_ref[...], modes)
    swap_across_plane(
        lambda b: rows_at(s3, 16 * b, 16),
        lambda b: rows_at(r3, 16 * b, 16),
        send_sem.at[3],
        recv_sem.at[3],
    )
    settle(r3, recv_sem.at[3])
    for a in range(16):
        for c in range(2):
            s4[c, 8 * a : 8 * a + 8, :] = r3[pl.ds(128 * c + a, 8, stride=16), :]
    swap_along_flow(
        lambda a: halves_at(s4, 8 * a, 8),
        lambda a: halves_at(r4, 8 * a, 8),
        send_sem.at[4],
        recv_sem.at[4],
    )
    settle(r4, recv_sem.at[4])
    half = [fdot(hy, r4[c]) for c in range(2)]
    plane = fdot(jnp.concatenate(half, axis=1), hz_ref[...])
    s5[0:128, :] = plane[:, :128]
    s5[128:256, :] = plane[:, 128:]
    swap_across_plane(
        lambda b: rows_at(s5, 16 * b, 16),
        lambda b: rows_at(r5, 16 * b, 16),
        send_sem.at[5],
        recv_sem.at[5],
    )
    settle(r5, recv_sem.at[5])

    ahead, behind = lax.rem(flow + 1, FLOW), lax.rem(flow + FLOW - 1, FLOW)
    above, below = lax.rem(cy + 1, CY), lax.rem(cy + CY - 1, CY)
    copies = []

    def halo(n, source, target, device):
        copies.append(
            pltpu.make_async_remote_copy(
                src_ref=source,
                dst_ref=target,
                send_sem=hsend_sem.at[n],
                recv_sem=hrecv_sem.at[n],
                device_id=device,
                device_id_type=MESH,
            )
        )
        copies[-1].start()

    halo(0, r5.at[pl.ds(240, 16), :], xh.at[pl.ds(0, 16), :], {"flow": ahead})
    halo(1, r5.at[pl.ds(0, 16), :], xh.at[pl.ds(16, 16), :], {"flow": behind})
    ys[0:16, :] = r5[pl.ds(15, 16, stride=16), :]
    ys[16:32, :] = r5[pl.ds(0, 16, stride=16), :]
    halo(2, ys.at[pl.ds(0, 16), :], yh.at[pl.ds(0, 16), :], {"cy": above})
    halo(3, ys.at[pl.ds(16, 16), :], yh.at[pl.ds(16, 16), :], {"cy": below})
    packed = [jnp.zeros((16, 128), f32), jnp.zeros((16, 128), f32)]
    lane = lax.broadcasted_iota(jnp.int32, (16, 128), 1)
    for x in range(16):
        at = 16 * (x // 2)
        moved = pltpu.roll(r5[16 * x : 16 * x + 16, :], (at + 1) % 128, 1)
        packed[x % 2] = jnp.where((lane == at) | (lane == at + 1), moved, packed[x % 2])
    zs[0:16, :] = packed[0]
    zs[16:32, :] = packed[1]
    halo(4, zs, zh, {"cz": 1 - cz})
    phi_out[...] = r5[...]
    for copy in copies:
        copy.wait()
    xh_out[...] = xh[...]
    yh_out[...] = yh[...]
    zh_out[...] = zh[...]
    for n, ref in enumerate((s0, s1, s2, s3, s4, s5)):
        if n in (1, 4):
            settle(ref.at[:, pl.ds(0, 120), :], send_sem.at[n])
        else:
            settle(ref.at[pl.ds(0, 240), :], send_sem.at[n])


def solve_potential(ion_pos, ion_neg):
    hx, hy, hz, lam = (jnp.asarray(t) for t in tables())
    rows = (256, 128)
    halves = (2, 128, 128)
    vmem = pl.BlockSpec(memory_space=pltpu.VMEM)
    anywhere = pl.BlockSpec(memory_space=pl.ANY)
    shapes = [rows, rows, (32, 128), (32, 128), (32, 128)]
    buffers = [rows, rows, halves, halves, rows, rows, rows, rows, halves, halves, rows, rows]
    buffers += [(32, 128)] * 5
    return pl.pallas_call(
        potential_kernel,
        out_shape=[jax.ShapeDtypeStruct(s, f32) for s in shapes],
        in_specs=[anywhere, anywhere, vmem, vmem, vmem, vmem],
        out_specs=[vmem] * 5,
        scratch_shapes=[pltpu.VMEM((14, 256, 128), f32)]
        + [pltpu.VMEM(s, f32) for s in buffers]
        + [
            pltpu.SemaphoreType.DMA((2,)),
            pltpu.SemaphoreType.DMA((6,)),
            pltpu.SemaphoreType.DMA((6,)),
            pltpu.SemaphoreType.DMA((5,)),
            pltpu.SemaphoreType.DMA((5,)),
        ],
        compiler_params=pltpu.CompilerParams(
            collective_id=0, has_side_effects=True, vmem_limit_bytes=40 << 20
        ),
        name="potential",
    )(ion_pos, ion_neg, hx, hy, hz, lam)


def pick_solid(gray, table_ref):
    bits = [(gray & (1 << n)) != 0 for n in range(4)]
    level = [table_ref[n] for n in range(16)]
    values = [jnp.where(bits[0], level[n + 1], level[n]) for n in range(0, 16, 2)]
    for n in range(1, 4):
        values = [
            jnp.where(bits[n], values[m + 1], values[m]) for m in range(0, len(values), 2)
        ]
    return values[0]


def fill_fields(phi, xh, yh, zh, field):
    lane = lax.broadcasted_iota(jnp.int32, (16, 128), 1)
    row = lax.broadcasted_iota(jnp.int32, (16, 128), 0)
    for x in range(16):
        here = phi[16 * x : 16 * x + 16, :]
        low = xh[0:16, :] if x == 0 else phi[16 * x - 16 : 16 * x, :]
        high = xh[16:32, :] if x == 15 else phi[16 * x + 16 : 16 * x + 32, :]
        field[0, 16 * x : 16 * x + 16, :] = -0.5 * (high - low)
        low = jnp.where(row == 0, yh[x : x + 1, :], pltpu.roll(here, 1, 0))
        high = jnp.where(row == 15, yh[16 + x : 17 + x, :], pltpu.roll(here, 15, 0))
        field[1, 16 * x : 16 * x + 16, :] = -0.5 * (high - low)
        edge = zh[16 * (x % 2) : 16 * (x % 2) + 16, :]
        at = 16 * (x // 2)
        low = jnp.where(lane == 0, pltpu.roll(edge, (128 - at) % 128, 1), pltpu.roll(here, 1, 1))
        high = jnp.where(
            lane == 127, pltpu.roll(edge, (127 - at - 1) % 128, 1), pltpu.roll(here, 127, 1)
        )
        field[2, 16 * x : 16 * x + 16, :] = -0.5 * (high - low)


def collide(f, g, h, gray, table_ref, field, emit):
    solid = pick_solid(gray, table_ref)
    conc_pos = sum(g[1:], g[0])
    conc_neg = sum(h[1:], h[0])
    charge = conc_pos - conc_neg
    density = sum(f[1:], f[0])
    inverse = 1.0 / density
    momentum = []
    for axis in range(3):
        plus = [f[q] for q in range(19) if flow_dirs[q][axis] == 1]
        minus = [f[q] for q in range(19) if flow_dirs[q][axis] == -1]
        momentum.append(sum(plus[1:], plus[0]) - sum(minus[1:], minus[0]))
    velocity = [m * inverse for m in momentum]
    push = (tau_flow * charge) * inverse
    drift = [velocity[d] + push * field[d] for d in range(3)]
    square = drift[0] * drift[0] + drift[1] * drift[1] + drift[2] * drift[2]
    omega = (1.0 - solid) * (1.0 / tau_flow)
    keep = 1.0 - omega - solid
    mass = omega * density
    base = 1.0 - 1.5 * square
    emit(0, (keep + solid) * f[0] + (mass * flow_weights[0]) * base)
    for q in range(1, 19, 2):
        along = None
        for d in range(3):
            if flow_dirs[q][d]:
                term = drift[d]
                if along is None:
                    along = term if flow_dirs[q][d] == 1 else -term
                else:
                    along = along + term if flow_dirs[q][d] == 1 else along - term
        scaled = mass * flow_weights[q]
        even = scaled * (base + 4.5 * along * along)
        odd = (3.0 * scaled) * along
        emit(q, keep * f[q] + solid * f[q + 1] + (even + odd))
        emit(q + 1, keep * f[q + 1] + solid * f[q] + (even - odd))
    omega = (1.0 - solid) * (1.0 / tau_ion)
    keep = 1.0 - omega - solid
    for start, pops, conc, sign in ((19, g, conc_pos, mobility), (26, h, conc_neg, -mobility)):
        mass = omega * conc
        emit(start, (keep + solid) * pops[0] + ion_weights[0] * mass)
        even = ion_weights[1] * mass
        for d in range(3):
            q = 1 + 2 * d
            odd = (4.0 * even) * (velocity[d] + sign * field[d])
            emit(start + q, keep * pops[q] + solid * pops[q + 1] + (even + odd))
            emit(start + q + 1, keep * pops[q + 1] + solid * pops[q] + (even - odd))


def collision_kernel(
    table_ref, flow_ref, pos_ref, neg_ref, gray_ref, phi, xh, yh, zh,
    post, xf, yf, zf, corner, field,
):
    fill_fields(phi, xh, yh, zh, field)

    def block(i, carry):
        at = pl.ds(pl.multiple_of(8 * i, 8), 8)

        def emit(q, values):
            post[q, at, :] = values

        collide(
            [flow_ref[q, at, :] for q in range(19)],
            [pos_ref[q, at, :] for q in range(7)],
            [neg_ref[q, at, :] for q in range(7)],
            gray_ref[at, :],
            table_ref,
            [field[d, at, :] for d in range(3)],
            emit,
        )
        return carry

    lax.fori_loop(0, 32, block, 0)
    gather_faces(post, xf, yf, zf, corner)


def gather_faces(post, xf, yf, zf, corner):
    for n, q in enumerate(FACE[0, 1]):
        xf[n] = post[q, 240:256, :]
    for n, q in enumerate(FACE[0, -1]):
        xf[7 + n] = post[q, 0:16, :]
    for n, q in enumerate(FACE[1, 1]):
        yf[n] = post[q, pl.ds(15, 16, stride=16), :]
    for n, q in enumerate(FACE[1, -1]):
        yf[7 + n] = post[q, pl.ds(0, 16, stride=16), :]
    lane = lax.broadcasted_iota(jnp.int32, (16, 128), 1)
    packed = [jnp.zeros((16, 128), f32), jnp.zeros((16, 128), f32)]
    for n, (up, down) in enumerate(zip(FACE[2, 1], FACE[2, -1])):
        for x in range(16):
            both = jnp.where(
                lane == 127, post[up, 16 * x : 16 * x + 16, :], post[down, 16 * x : 16 * x + 16, :]
            )
            at = 16 * (x // 2) + 2 * n
            moved = pltpu.roll(both, (at + 1) % 128, 1)
            packed[x % 2] = jnp.where((lane == at) | (lane == at + 1), moved, packed[x % 2])
    zf[0:16, :] = packed[0]
    zf[16:32, :] = packed[1]
    corner[0] = post[7, 248:256, :]
    corner[1] = post[8, 0:8, :]
    corner[2] = post[9, 240:248, :]
    corner[3] = post[10, 8:16, :]


def collide_all(table, flow_pops, ion_pos, ion_neg, gray, phi, xh, yh, zh):
    vmem = pl.BlockSpec(memory_space=pltpu.VMEM)
    shapes = [(33, 256, 128), (14, 16, 128), (14, 16, 128), (32, 128), (4, 8, 128)]
    return pl.pallas_call(
        collision_kernel,
        out_shape=[jax.ShapeDtypeStruct(s, f32) for s in shapes],
        in_specs=[pl.BlockSpec(memory_space=pltpu.SMEM)] + [vmem] * 8,
        out_specs=[vmem] * 5,
        scratch_shapes=[pltpu.VMEM((3, 256, 128), f32)],
        compiler_params=pltpu.CompilerParams(vmem_limit_bytes=40 << 20),
        name="collision",
    )(table, flow_pops, ion_pos, ion_neg, gray, phi, xh, yh, zh)


def face_messages(xf, yf, zf, corner, xr, yr, zr, zx, zy, cr):
    up, down = pl.ds(0, 7), pl.ds(7, 7)
    low, high = pl.ds(0, 16), pl.ds(16, 16)
    return [
        (xf.at[up], xr.at[up], 1, 0, 0),
        (xf.at[down], xr.at[down], -1, 0, 0),
        (yf.at[up], yr.at[up], 0, 1, 0),
        (yf.at[down], yr.at[down], 0, -1, 0),
        (zf, zr, 0, 0, 1),
        (zf.at[high], zx.at[low], 1, 0, 1),
        (zf.at[low], zx.at[high], -1, 0, 1),
        (zf, zy.at[0], 0, 1, 1),
        (zf, zy.at[1], 0, -1, 1),
        (corner.at[0], cr.at[0], 1, 1, 0),
        (corner.at[1], cr.at[1], -1, -1, 0),
        (corner.at[2], cr.at[2], 1, -1, 0),
        (corner.at[3], cr.at[3], -1, 1, 0),
    ]


def partner(step_flow, step_cy, cross):
    flow, cy, cz = place()
    return (
        lax.rem(flow + FLOW + step_flow, FLOW),
        lax.rem(cy + CY + step_cy, CY),
        1 - cz if cross else cz,
    )


def faces_kernel(
    xf, yf, zf, corner, xo, yo, zo, zxo, zyo, co, xr, yr, zr, zx, zy, cr, send_sem, recv_sem
):
    messages = face_messages(xf, yf, zf, corner, xr, yr, zr, zx, zy, cr)
    barrier = pltpu.get_barrier_semaphore()
    for _, _, i, j, k in messages:
        pl.semaphore_signal(barrier, inc=1, device_id=partner(i, j, k), device_id_type=MESH)
    pl.semaphore_wait(barrier, len(messages))
    copies = []
    for n, (source, target, i, j, k) in enumerate(messages):
        copies.append(
            pltpu.make_async_remote_copy(
                src_ref=source,
                dst_ref=target,
                send_sem=send_sem.at[n],
                recv_sem=recv_sem.at[n],
                device_id=partner(i, j, k),
                device_id_type=MESH,
            )
        )
        copies[-1].start()
    for copy in copies:
        copy.wait()
    for out, got in ((xo, xr), (yo, yr), (zo, zr), (zxo, zx), (zyo, zy), (co, cr)):
        out[...] = got[...]


def swap_faces(xf, yf, zf, corner):
    vmem = pl.BlockSpec(memory_space=pltpu.VMEM)
    shapes = [(14, 16, 128), (14, 16, 128), (32, 128), (32, 128), (2, 32, 128), (4, 8, 128)]
    return pl.pallas_call(
        faces_kernel,
        out_shape=[jax.ShapeDtypeStruct(s, f32) for s in shapes],
        in_specs=[vmem] * 4,
        out_specs=[vmem] * 6,
        scratch_shapes=[pltpu.VMEM(s, f32) for s in shapes]
        + [pltpu.SemaphoreType.DMA((13,)), pltpu.SemaphoreType.DMA((13,))],
        compiler_params=pltpu.CompilerParams(
            collective_id=1, has_side_effects=True, vmem_limit_bytes=8 << 20
        ),
        name="faces",
    )(xf, yf, zf, corner)


def run_population(q, load, xr, yr, zr, zx, zy, cr, store):
    ex, ey, ez = DIRS[q]
    lane = lax.broadcasted_iota(jnp.int32, (16, 128), 1)
    row = lax.broadcasted_iota(jnp.int32, (16, 128), 0)
    last_row, first_row = (15, 0) if ey == 1 else (0, 15)
    for x in range(16):
        xs = x - ex
        outside = xs < 0 or xs > 15
        if outside:
            plane = xr[FACE[0, ex].index(q) + (0 if ex == 1 else 7)]
        else:
            plane = load(xs)
        if ey:
            if outside:
                n = {7: 0, 8: 1, 9: 2, 10: 3}[q]
                tile = 7 if ey == 1 else 0
                line = cr[n, tile : tile + 1, :]
            else:
                line = yr[FACE[1, ey].index(q) + (0 if ey == 1 else 7), xs : xs + 1, :]
            plane = jnp.where(row == first_row, line, pltpu.roll(plane, ey % 16, 0))
        if ez:
            face = FACE[2, ez].index(q)
            if outside:
                edge = zx[0:16, :] if ex == 1 else zx[16:32, :]
                block = 7 if ex == 1 else 0
            else:
                edge = zr[16 * (xs % 2) : 16 * (xs % 2) + 16, :]
                block = xs // 2
            at = 16 * block + 2 * face + (0 if ez == 1 else 1)
            if ey:
                beyond = zy[0 if ey == 1 else 1, 16 * (xs % 2) : 16 * (xs % 2) + 16, :]
                edge = pltpu.roll(jnp.where(row == last_row, beyond, edge), ey % 16, 0)
            goal = 0 if ez == 1 else 127
            moved = pltpu.roll(edge, (goal - at) % 128, 1) if (goal - at) % 128 else edge
            plane = jnp.where(lane == goal, moved, pltpu.roll(plane, ez % 128, 1))
        store(x, plane)


def running_kernel(post, xr, yr, zr, zx, zy, cr, flow_out, pos_out, neg_out, got, moved, in_sem, out_sem):
    def output(q):
        if q < 19:
            return flow_out.at[q]
        return pos_out.at[q - 19] if q < 26 else neg_out.at[q - 26]

    reads = [pltpu.make_async_copy(post.at[q], got.at[q], in_sem.at[q]) for q in range(33)]
    writes = []
    for copy in reads:
        copy.start()
    for q in range(33):
        reads[q].wait()
        if q in (0, 19, 26):
            writes.append(pltpu.make_async_copy(got.at[q], output(q), out_sem.at[q]))
        else:

            def load(x, q=q):
                return got[q, 16 * x : 16 * x + 16, :]

            def store(x, plane, q=q):
                moved[q, 16 * x : 16 * x + 16, :] = plane

            run_population(q, load, xr, yr, zr, zx, zy, cr, store)
            writes.append(pltpu.make_async_copy(moved.at[q], output(q), out_sem.at[q]))
        writes[-1].start()
    for copy in writes:
        copy.wait()


def run_all(post, faces):
    vmem = pl.BlockSpec(memory_space=pltpu.VMEM)
    anywhere = pl.BlockSpec(memory_space=pl.ANY)
    return pl.pallas_call(
        running_kernel,
        out_shape=[jax.ShapeDtypeStruct((n, 256, 128), f32) for n in (19, 7, 7)],
        in_specs=[anywhere] + [vmem] * 6,
        out_specs=[anywhere] * 3,
        scratch_shapes=[
            pltpu.VMEM((33, 256, 128), f32),
            pltpu.VMEM((33, 256, 128), f32),
            pltpu.SemaphoreType.DMA((33,)),
            pltpu.SemaphoreType.DMA((33,)),
        ],
        compiler_params=pltpu.CompilerParams(vmem_limit_bytes=40 << 20),
        name="running",
    )(post, *faces)


def shards(flow_pops, ion_pos, ion_neg, gray_class, fraction_table):
    extent = gray_class.shape
    flow_pops = flow_pops.reshape(19, 256, 128)
    ion_pos = ion_pos.reshape(7, 256, 128)
    ion_neg = ion_neg.reshape(7, 256, 128)
    gray = gray_class.reshape(256, 128)
    _, phi, xh, yh, zh = solve_potential(ion_pos, ion_neg)
    post, *faces = collide_all(
        fraction_table, flow_pops, ion_pos, ion_neg, gray, phi, xh, yh, zh
    )
    flow_new, pos_new, neg_new = run_all(post, swap_faces(*faces))
    return (
        flow_new.reshape(19, *extent),
        pos_new.reshape(7, *extent),
        neg_new.reshape(7, *extent),
        phi.reshape(extent),
    )


def solution(mesh):
    in_specs = (
        P(None, "flow", "cy", "cz"),
        P(None, "flow", "cy", "cz"),
        P(None, "flow", "cy", "cz"),
        P("flow", "cy", "cz"),
        P(),
    )
    out_specs = (
        P(None, "flow", "cy", "cz"),
        P(None, "flow", "cy", "cz"),
        P(None, "flow", "cy", "cz"),
        P("flow", "cy", "cz"),
    )
    return jax.shard_map(shards, mesh=mesh, in_specs=in_specs, out_specs=out_specs, check_vma=False)
```

profile of v0, /device:TPU:1, one launch (start us, length us, event | category | flops | bytes accessed | tf_op | source)
XLA Modules:
  0.0 81.5 jit_solution(9879777888712180212)
XLA Ops:
  0.6 0.0 copy-start.8
  0.6 0.0 copy-start
  0.7 1.2 %copy-done = f32[7,16,16,128]{3,2,1,0:T(8,128)S(1)} copy-done((f32[7,16,16,128]{3,2,1,0:T(8,128)S(1)}, f32[7,16,16,128]{3,2,1,0:T(8,128)}, u32[]{:S(2)}) %copy-start) | copy-done | bytes 917528
  1.8 0.0 copy-start.1
  1.8 1.2 %copy-done.1 = f32[7,16,16,128]{3,2,1,0:T(8,128)S(1)} copy-done((f32[7,16,16,128]{3,2,1,0:T(8,128)S(1)}, f32[7,16,16,128]{3,2,1,0:T(8,128)}, u32[]{:S(2)}) %copy-start.1) | copy-done | bytes 917528
  3.0 0.0 copy-start.3
  3.0 0.9 %copy-done.3 = f32[256,256]{1,0:T(8,128)S(1)} copy-done((f32[256,256]{1,0:T(8,128)S(1)}, f32[256,256]{1,0:T(8,128)}, u32[]{:S(2)}) %copy-start.3) | copy-done | bytes 262168
  4.0 0.0 copy-start.4
  4.0 0.9 %copy-done.4 = f32[256,256]{1,0:T(8,128)S(1)} copy-done((f32[256,256]{1,0:T(8,128)S(1)}, f32[256,256]{1,0:T(8,128)}, u32[]{:S(2)}) %copy-start.4) | copy-done | bytes 262168
  4.9 0.0 copy-start.5
  4.9 0.9 %copy-done.5 = f32[392,128]{1,0:T(8,128)S(1)} copy-done((f32[392,128]{1,0:T(8,128)S(1)}, f32[392,128]{1,0:T(8,128)}, u32[]{:S(2)}) %copy-start.5) | copy-done | bytes 200728
  5.8 0.0 copy-start.7
  5.8 0.8 %copy-done.7 = f32[128,128]{1,0:T(8,128)S(1)} copy-done((f32[128,128]{1,0:T(8,128)S(1)}, f32[128,128]{1,0:T(8,128)}, u32[]{:S(2)}) %copy-start.7) | copy-done | bytes 65560
  6.7 0.0 copy-start.2
  6.7 0.0 copy-start.6
  6.7 50.7 %potential.1 = (f32[256,128]{1,0:T(8,128)}, f32[256,128]{1,0:T(8,128)S(1)}, f32[32,128]{1,0:T(8,128)S(1)}, f32[32,128]{1,0:T(8,128)S(1)}, f32[32,128]{1,0:T(8,128)S(1)}) custom-call(f32[7,256,128]{2,1,0:T(8,128)S(1)} %bitcast.8, f32[7,256,128]{2,1,0:T(8,128)S(1)} %bitcast.10, f32[256,256]{1,0:T(8,128)S(1)} %copy-done.4, f32[128,128]{1,0:T(8,128)S(1)} %copy-done.7, ...), custom_call_target="tpu_custom_call" | custom-call | tf_op jit(solution)/shard_map/potential/pallas_call | solution.py:330
  57.4 0.0 copy-done.8
  57.4 0.0 copy-done.2
  57.5 0.0 copy-done.6
  57.5 3.3 %collision.1 = (f32[33,256,128]{2,1,0:T(8,128)S(1)}, f32[14,16,128]{2,1,0:T(8,128)S(1)}, f32[14,16,128]{2,1,0:T(8,128)S(1)}, f32[32,128]{1,0:T(8,128)S(1)}, f32[4,8,128]{2,1,0:T(8,128)S(1)}) custom-call(f32[16]{0:T(128)S(1)} %copy-done.8, f32[19,256,128]{2,1,0:T(8,128)S(1)} %bitcast.12, f32[7,256,128]{2,1,0:T(8,128)S(1)} %bitcast.9, ...), custom_call_target="tpu_custom_call" | custom-call | tf_op jit(solution)/shard_map/collision/pallas_call | solution.py:487
  60.8 11.1 %faces.1 = (f32[14,16,128]{2,1,0:T(8,128)S(1)}, f32[14,16,128]{2,1,0:T(8,128)S(1)}, f32[32,128]{1,0:T(8,128)S(1)}, f32[32,128]{1,0:T(8,128)S(1)}, f32[2,32,128]{2,1,0:T(8,128)S(1)}, /*index=5*/f32[4,8,128]{2,1,0:T(8,128)S(1)}) custom-call(f32[14,16,128]{2,1,0:T(8,128)S(1)} %get-tuple-element.27.xf, f32[14,16,128]{2,1,0:T(8,128)S(1)} %get-tuple-element.28.yf, ...), custom_call_target="tpu_custom_call" | custom-call | tf_op jit(solution)/shard_map/faces/pallas_call | solution.py:557
  71.9 9.0 %running.1 = (f32[19,256,128]{2,1,0:T(8,128)}, f32[7,256,128]{2,1,0:T(8,128)}, f32[7,256,128]{2,1,0:T(8,128)}) custom-call(f32[33,256,128]{2,1,0:T(8,128)S(1)} %get-tuple-element.26.post, f32[14,16,128]{2,1,0:T(8,128)S(1)} %get-tuple-element.31.xr, f32[14,16,128]{2,1,0:T(8,128)S(1)} %get-tuple-element.32.yr, f32[32,128]{1,0:T(8,128)S(1)} %get-tuple-element.33.zr, ...), custom_call_target="tpu_custom_call" | custom-call | tf_op jit(solution)/shard_map/running/pallas_call | solution.py:641
  80.9 0.7 copy.14
Async XLA Ops:
  0.6 56.8 %copy-start.8 = (f32[16]{0:T(128)S(1)}, f32[16]{0:T(128)}, u32[]{:S(2)}) copy-start(f32[16]{0:T(128)} %table_ref.1) | copy-start | bytes 196
  0.6 1.2 %copy-start = (f32[7,16,16,128]{3,2,1,0:T(8,128)S(1)}, f32[7,16,16,128]{3,2,1,0:T(8,128)}, u32[]{:S(2)}) copy-start(f32[7,16,16,128]{3,2,1,0:T(8,128)} %param.10) | copy-start | bytes 2752516
  1.8 1.2 %copy-start.1 = (f32[7,16,16,128]{3,2,1,0:T(8,128)S(1)}, f32[7,16,16,128]{3,2,1,0:T(8,128)}, u32[]{:S(2)}) copy-start(f32[7,16,16,128]{3,2,1,0:T(8,128)} %param.11) | copy-start | bytes 2752516
  3.0 0.9 %copy-start.3 = (f32[256,256]{1,0:T(8,128)S(1)}, f32[256,256]{1,0:T(8,128)}, u32[]{:S(2)}) copy-start(f32[256,256]{1,0:T(8,128)} %constant.10.clone.hz_ref) | copy-start | bytes 786436
  4.0 0.9 %copy-start.4 = (f32[256,256]{1,0:T(8,128)S(1)}, f32[256,256]{1,0:T(8,128)}, u32[]{:S(2)}) copy-start(f32[256,256]{1,0:T(8,128)} %constant.8.clone.hx_ref) | copy-start | bytes 786436
  4.9 0.9 %copy-start.5 = (f32[392,128]{1,0:T(8,128)S(1)}, f32[392,128]{1,0:T(8,128)}, u32[]{:S(2)}) copy-start(f32[392,128]{1,0:T(8,128)} %constant.11.clone.lam_ref) | copy-start | bytes 602116
  5.8 0.8 %copy-start.7 = (f32[128,128]{1,0:T(8,128)S(1)}, f32[128,128]{1,0:T(8,128)}, u32[]{:S(2)}) copy-start(f32[128,128]{1,0:T(8,128)} %constant.9.clone.hy_ref) | copy-start | bytes 196612
  6.7 50.8 %copy-start.2 = (f32[19,16,16,128]{3,2,1,0:T(8,128)S(1)}, f32[19,16,16,128]{3,2,1,0:T(8,128)}, u32[]{:S(2)}) copy-start(f32[19,16,16,128]{3,2,1,0:T(8,128)} %param.9) | copy-start | bytes 7471108
  6.7 50.8 %copy-start.6 = (s32[16,16,128]{2,1,0:T(8,128)S(1)}, s32[16,16,128]{2,1,0:T(8,128)}, u32[]{:S(2)}) copy-start(s32[16,16,128]{2,1,0:T(8,128)} %param.12) | copy-start | bytes 393220
where the time goes:
time: 81.8 us; the launch traced here: 81.5 us
  Pallas kernels  74.1 us (91%)
  local copies, waits for them, and re-layouts  6.69 us (8%)
    pallas_call x1, Pallas kernels, solve_potential(): pl.pallas_call(potential_kernel, out_shape=[jax.ShapeDtypeStruct(s, f32)...  50.7 us
    pallas_call x1, Pallas kernels, swap_faces(): pl.pallas_call(faces_kernel, out_shape=[jax.ShapeDtypeStruct(s, f32) for...  11.1 us
    pallas_call x1, Pallas kernels, run_all(): pl.pallas_call(running_kernel, out_shape=[jax.ShapeDtypeStruct((n, 256, 1...  8.99 us
    unnamed x19, local copies, waits for them, and re-layouts  6.69 us
    pallas_call x1, Pallas kernels, collide_all(): pl.pallas_call(collision_kernel, out_shape=[jax.ShapeDtypeStruct(s, f32)...  3.29 us

commit v1 on v0

v1 whole, which is shorter than its diff:
```python
import functools
import math

import jax
import jax.numpy as jnp
import numpy as np
from jax import lax
from jax.experimental import pallas as pl
from jax.experimental.pallas import tpu as pltpu
from jax.sharding import PartitionSpec as P

flow_dirs = (
    (0, 0, 0),
    (1, 0, 0),
    (-1, 0, 0),
    (0, 1, 0),
    (0, -1, 0),
    (0, 0, 1),
    (0, 0, -1),
    (1, 1, 0),
    (-1, -1, 0),
    (1, -1, 0),
    (-1, 1, 0),
    (1, 0, 1),
    (-1, 0, -1),
    (1, 0, -1),
    (-1, 0, 1),
    (0, 1, 1),
    (0, -1, -1),
    (0, 1, -1),
    (0, -1, 1),
)
flow_weights = (1.0 / 3.0,) + (1.0 / 18.0,) * 6 + (1.0 / 36.0,) * 12
ion_weights = (0.25,) + (0.125,) * 6
tau_flow = 0.8
tau_ion = 0.9
coupling = 2.0
mobility = 0.5
NX, NY, NZ = 256, 128, 256
FLOW, CY, CZ = 16, 8, 2
MESH = pl.DeviceIdType.MESH
f32 = jnp.float32
VMEM_LIMIT = 60 << 20

DIRS = flow_dirs + flow_dirs[:7] + flow_dirs[:7]
FACE = {
    (axis, sign): [q for q in range(33) if DIRS[q][axis] == sign]
    for axis in range(3)
    for sign in (1, -1)
}


def cas_table(points_k, points_n, length):
    product = (points_k[:, None].astype(np.int64) * points_n[None, :]) % length
    angle = product * (2.0 * math.pi / length)
    return (np.cos(angle) + np.sin(angle)).astype(np.float32)


def tables():
    order = np.array([16 * a + b for b in range(16) for a in range(16)])
    hx = cas_table(order, order, NX)
    hy = cas_table(np.arange(NY), np.arange(NY), NY)
    hz = cas_table(np.arange(NZ), np.arange(NZ), NZ)

    def lam(modes, length):
        return 4.0 * np.sin(np.pi * modes / length) ** 2

    rows = np.zeros((NX + NY + 8, 128))
    rows[:NX] = lam(order, NX)[:, None]
    rows[NX : NX + NY] = lam(np.arange(NY), NY)[:, None]
    rows[NX + NY : NX + NY + 2] = lam(np.arange(NZ), NZ).reshape(2, 128)
    return hx, hy, hz, rows.astype(np.float32)


def place():
    return lax.axis_index("flow"), lax.axis_index("cy"), lax.axis_index("cz")


def fdot(left, right):
    return jnp.dot(left, right, precision=lax.Precision.HIGHEST, preferred_element_type=f32)


def settle(ref, sem):
    pltpu.make_async_copy(ref, ref, sem).wait()


def column_mask(shape, index):
    return lax.broadcasted_iota(jnp.int32, shape, 1) == index


def row_mask(shape, index):
    return lax.broadcasted_iota(jnp.int32, shape, 0) == index


def swap_across_plane(source, target, send_sem, recv_sem):
    _, cy, cz = place()
    me = cz * CY + cy

    def step(k, carry):
        other = lax.rem(me + k, 16)
        pltpu.make_async_remote_copy(
            src_ref=source(other),
            dst_ref=target(me),
            send_sem=send_sem,
            recv_sem=recv_sem,
            device_id={"cy": lax.rem(other, CY), "cz": lax.div(other, CY)},
            device_id_type=MESH,
        ).start()
        return carry

    lax.fori_loop(1, 16, step, 0)
    pltpu.make_async_copy(source(me), target(me), recv_sem).start()


def swap_along_flow(source, target, send_sem, recv_sem):
    me, _, _ = place()

    def step(k, carry):
        other = lax.rem(me + k, 16)
        pltpu.make_async_remote_copy(
            src_ref=source(other),
            dst_ref=target(me),
            send_sem=send_sem,
            recv_sem=recv_sem,
            device_id={"flow": other},
            device_id_type=MESH,
        ).start()
        return carry

    lax.fori_loop(1, 16, step, 0)
    pltpu.make_async_copy(source(me), target(me), recv_sem).start()


def rows_at(ref, start, count):
    return ref.at[pl.ds(pl.multiple_of(start, count), count), :]


def halves_at(ref, start, count):
    return ref.at[:, pl.ds(pl.multiple_of(start, count), count), :]


def pick_solid(gray, table_ref):
    bits = [(gray & (1 << n)) != 0 for n in range(4)]
    level = [table_ref[n] for n in range(16)]
    values = [jnp.where(bits[0], level[n + 1], level[n]) for n in range(0, 16, 2)]
    for n in range(1, 4):
        values = [
            jnp.where(bits[n], values[m + 1], values[m]) for m in range(0, len(values), 2)
        ]
    return values[0]


def fill_fields(phi, xh, yh, zh, field):
    lane = lax.broadcasted_iota(jnp.int32, (16, 128), 1)
    row = lax.broadcasted_iota(jnp.int32, (16, 128), 0)
    for x in range(16):
        here = phi[16 * x : 16 * x + 16, :]
        low = xh[0:16, :] if x == 0 else phi[16 * x - 16 : 16 * x, :]
        high = xh[16:32, :] if x == 15 else phi[16 * x + 16 : 16 * x + 32, :]
        field[0, 16 * x : 16 * x + 16, :] = -0.5 * (high - low)
        low = jnp.where(row == 0, yh[x : x + 1, :], pltpu.roll(here, 1, 0))
        high = jnp.where(row == 15, yh[16 + x : 17 + x, :], pltpu.roll(here, 15, 0))
        field[1, 16 * x : 16 * x + 16, :] = -0.5 * (high - low)
        edge = zh[16 * (x % 2) : 16 * (x % 2) + 16, :]
        at = 16 * (x // 2)
        low = jnp.where(lane == 0, pltpu.roll(edge, (128 - at) % 128, 1), pltpu.roll(here, 1, 1))
        high = jnp.where(
            lane == 127, pltpu.roll(edge, (127 - at - 1) % 128, 1), pltpu.roll(here, 127, 1)
        )
        field[2, 16 * x : 16 * x + 16, :] = -0.5 * (high - low)


def prepare(pops, charge, gray, table_ref, aux):
    def block(i, carry):
        at = pl.ds(pl.multiple_of(8 * i, 8), 8)
        f = [pops[q, at, :] for q in range(33)]
        solid = pick_solid(gray[at, :], table_ref)
        density = sum(f[1:19], f[0])
        inverse = 1.0 / density
        for axis in range(3):
            plus = [f[q] for q in range(19) if flow_dirs[q][axis] == 1]
            minus = [f[q] for q in range(19) if flow_dirs[q][axis] == -1]
            aux[axis, at, :] = (sum(plus[1:], plus[0]) - sum(minus[1:], minus[0])) * inverse
        aux[3, at, :] = (tau_flow * charge[at, :]) * inverse
        omega = (1.0 - solid) * (1.0 / tau_flow)
        keep = 1.0 - omega - solid
        aux[4, at, :] = omega * density
        pops[0, at, :] = (keep + solid) * f[0]
        for q in range(1, 19, 2):
            pops[q, at, :] = keep * f[q] + solid * f[q + 1]
            pops[q + 1, at, :] = keep * f[q + 1] + solid * f[q]
        omega = (1.0 - solid) * (1.0 / tau_ion)
        keep = 1.0 - omega - solid
        for n, start in enumerate((19, 26)):
            g = f[start : start + 7]
            aux[5 + n, at, :] = omega * sum(g[1:], g[0])
            pops[start, at, :] = (keep + solid) * g[0]
            for q in range(1, 7, 2):
                pops[start + q, at, :] = keep * g[q] + solid * g[q + 1]
                pops[start + q + 1, at, :] = keep * g[q + 1] + solid * g[q]
        return carry

    lax.fori_loop(0, 32, block, 0)


def finish(pops, aux, field, post):
    def block(i, carry):
        at = pl.ds(pl.multiple_of(8 * i, 8), 8)
        velocity = [aux[d, at, :] for d in range(3)]
        electric = [field[d, at, :] for d in range(3)]
        push = aux[3, at, :]
        drift = [velocity[d] + push * electric[d] for d in range(3)]
        square = drift[0] * drift[0] + drift[1] * drift[1] + drift[2] * drift[2]
        mass = aux[4, at, :]
        base = 1.0 - 1.5 * square
        post[0, at, :] = pops[0, at, :] + (mass * flow_weights[0]) * base
        for q in range(1, 19, 2):
            along = None
            for d in range(3):
                if flow_dirs[q][d] and along is None:
                    along = drift[d] if flow_dirs[q][d] == 1 else -drift[d]
                elif flow_dirs[q][d]:
                    along = along + drift[d] if flow_dirs[q][d] == 1 else along - drift[d]
            scaled = mass * flow_weights[q]
            even = scaled * (base + 4.5 * along * along)
            odd = (3.0 * scaled) * along
            post[q, at, :] = pops[q, at, :] + (even + odd)
            post[q + 1, at, :] = pops[q + 1, at, :] + (even - odd)
        for start, n, sign in ((19, 5, mobility), (26, 6, -mobility)):
            mass = aux[n, at, :]
            post[start, at, :] = pops[start, at, :] + ion_weights[0] * mass
            even = ion_weights[1] * mass
            for d in range(3):
                q = start + 1 + 2 * d
                odd = (4.0 * even) * (velocity[d] + sign * electric[d])
                post[q, at, :] = pops[q, at, :] + (even + odd)
                post[q + 1, at, :] = pops[q + 1, at, :] + (even - odd)
        return carry

    lax.fori_loop(0, 32, block, 0)


def gather_faces(post, xf, yf, zf, corner):
    for n, q in enumerate(FACE[0, 1]):
        xf[n] = post[q, 240:256, :]
    for n, q in enumerate(FACE[0, -1]):
        xf[7 + n] = post[q, 0:16, :]
    for n, q in enumerate(FACE[1, 1]):
        yf[n] = post[q, pl.ds(15, 16, stride=16), :]
    for n, q in enumerate(FACE[1, -1]):
        yf[7 + n] = post[q, pl.ds(0, 16, stride=16), :]
    lane = lax.broadcasted_iota(jnp.int32, (16, 128), 1)
    packed = [jnp.zeros((16, 128), f32), jnp.zeros((16, 128), f32)]
    for n, (up, down) in enumerate(zip(FACE[2, 1], FACE[2, -1])):
        for x in range(16):
            both = jnp.where(
                lane == 127, post[up, 16 * x : 16 * x + 16, :], post[down, 16 * x : 16 * x + 16, :]
            )
            at = 16 * (x // 2) + 2 * n
            moved = pltpu.roll(both, (at + 1) % 128, 1)
            packed[x % 2] = jnp.where((lane == at) | (lane == at + 1), moved, packed[x % 2])
    zf[0:16, :] = packed[0]
    zf[16:32, :] = packed[1]
    corner[0] = post[7, 248:256, :]
    corner[1] = post[8, 0:8, :]
    corner[2] = post[9, 240:248, :]
    corner[3] = post[10, 8:16, :]


def face_messages(xf, yf, zf, corner, xr, yr, zr, zx, zy, cr):
    up, down = pl.ds(0, 7), pl.ds(7, 7)
    low, high = pl.ds(0, 16), pl.ds(16, 16)
    return [
        (xf.at[up], xr.at[up], 1, 0, 0),
        (xf.at[down], xr.at[down], -1, 0, 0),
        (yf.at[up], yr.at[up], 0, 1, 0),
        (yf.at[down], yr.at[down], 0, -1, 0),
        (zf, zr, 0, 0, 1),
        (zf.at[high], zx.at[low], 1, 0, 1),
        (zf.at[low], zx.at[high], -1, 0, 1),
        (zf, zy.at[0], 0, 1, 1),
        (zf, zy.at[1], 0, -1, 1),
        (corner.at[0], cr.at[0], 1, 1, 0),
        (corner.at[1], cr.at[1], -1, -1, 0),
        (corner.at[2], cr.at[2], 1, -1, 0),
        (corner.at[3], cr.at[3], -1, 1, 0),
    ]


def partner(step_flow, step_cy, cross):
    flow, cy, cz = place()
    return (
        lax.rem(flow + FLOW + step_flow, FLOW),
        lax.rem(cy + CY + step_cy, CY),
        1 - cz if cross else cz,
    )


FACE_SHAPES = [(14, 16, 128), (14, 16, 128), (32, 128), (32, 128), (2, 32, 128), (4, 8, 128)]


def main_kernel(
    table_ref, pos_hbm, neg_hbm, flow_hbm, gray_hbm, hx_hbm, hy_hbm, hz_hbm, lam_hbm,
    post_out, phi_out, xo, yo, zo, zxo, zyo, co,
    pops, post, gray, hx_ref, hy_ref, hz_ref, lam_ref, aux, field,
    s0, r0, s1, r1, s2, r2, s3, r3, s4, r4, s5, r5, ys, zs, xh, yh, zh,
    xf, yf, zf, corner, xr, yr, zr, zx, zy, cr,
    load_sem, send_sem, recv_sem, hsend_sem, hrecv_sem, fsend_sem, frecv_sem, store_sem,
):
    flow, cy, cz = place()
    loads = [
        pltpu.make_async_copy(source, target, load_sem.at[n])
        for n, (source, target) in enumerate(
            (
                (pos_hbm, pops.at[pl.ds(19, 7)]),
                (neg_hbm, pops.at[pl.ds(26, 7)]),
                (hy_hbm, hy_ref),
                (hz_hbm, hz_ref),
                (flow_hbm, pops.at[pl.ds(0, 19)]),
                (gray_hbm, gray),
                (hx_hbm, hx_ref),
                (lam_hbm, lam_ref),
            )
        )
    ]
    for copy in loads:
        copy.start()
    barrier = pltpu.get_barrier_semaphore()
    me = cz * CY + cy

    def greet(k, carry):
        other = lax.rem(me + k, 16)
        pl.semaphore_signal(
            barrier,
            inc=1,
            device_id={"cy": lax.rem(other, CY), "cz": lax.div(other, CY)},
            device_id_type=MESH,
        )
        pl.semaphore_signal(
            barrier, inc=1, device_id={"flow": lax.rem(flow + k, 16)}, device_id_type=MESH
        )
        return carry

    lax.fori_loop(1, 16, greet, 0)
    messages = face_messages(xf, yf, zf, corner, xr, yr, zr, zx, zy, cr)
    strangers = [m[2:] for m in messages if m[2] and (m[3] or m[4])]
    for i, j, k in strangers:
        pl.semaphore_signal(barrier, inc=1, device_id=partner(i, j, k), device_id_type=MESH)
    loads[0].wait()
    loads[1].wait()
    pos = pops[19]
    neg = pops[26]
    for q in range(1, 7):
        pos = pos + pops[19 + q]
        neg = neg + pops[26 + q]
    s0[...] = pos - neg
    pl.semaphore_wait(barrier, 30 + len(strangers))

    swap_across_plane(
        lambda b: rows_at(s0, 16 * b, 16),
        lambda b: rows_at(r0, 16 * b, 16),
        send_sem.at[0],
        recv_sem.at[0],
    )
    for copy in loads[2:]:
        copy.wait()
    prepare(pops, s0, gray, table_ref, aux)
    settle(r0, recv_sem.at[0])
    hy = hy_ref[...]
    half = [fdot(hy, r0[128 * c : 128 * c + 128, :]) for c in range(2)]
    spectrum = fdot(jnp.concatenate(half, axis=1), hz_ref[...])
    s1[0] = spectrum[:, :128]
    s1[1] = spectrum[:, 128:]
    swap_along_flow(
        lambda a: halves_at(s1, 8 * a, 8),
        lambda a: halves_at(r1, 8 * a, 8),
        send_sem.at[1],
        recv_sem.at[1],
    )
    settle(r1, recv_sem.at[1])
    for b in range(16):
        s2[16 * b : 16 * b + 16, :] = r1[b // CY, pl.ds(b % CY, 16, stride=8), :]
    swap_across_plane(
        lambda b: rows_at(s2, 16 * b, 16),
        lambda b: rows_at(r2, 16 * b, 16),
        send_sem.at[2],
        recv_sem.at[2],
    )
    total = (
        lam_ref[0:NX, :]
        + lam_ref[pl.ds(NX + CY * flow + cy, 1), :]
        + lam_ref[pl.ds(NX + NY + cz, 1), :]
    )
    scale = coupling / (NX * NY * NZ)
    green = jnp.where(total > 0.0, scale / jnp.where(total > 0.0, total, 1.0), 0.0)
    settle(r2, recv_sem.at[2])
    modes = green * fdot(hx_ref[...], r2[...])
    s3[...] = fdot(hx_ref[...], modes)
    swap_across_plane(
        lambda b: rows_at(s3, 16 * b, 16),
        lambda b: rows_at(r3, 16 * b, 16),
        send_sem.at[3],
        recv_sem.at[3],
    )
    settle(r3, recv_sem.at[3])
    for a in range(16):
        for c in range(2):
            s4[c, 8 * a : 8 * a + 8, :] = r3[pl.ds(128 * c + a, 8, stride=16), :]
    swap_along_flow(
        lambda a: halves_at(s4, 8 * a, 8),
        lambda a: halves_at(r4, 8 * a, 8),
        send_sem.at[4],
        recv_sem.at[4],
    )
    settle(r4, recv_sem.at[4])
    half = [fdot(hy, r4[c]) for c in range(2)]
    plane = fdot(jnp.concatenate(half, axis=1), hz_ref[...])
    s5[0:128, :] = plane[:, :128]
    s5[128:256, :] = plane[:, 128:]
    swap_across_plane(
        lambda b: rows_at(s5, 16 * b, 16),
        lambda b: rows_at(r5, 16 * b, 16),
        send_sem.at[5],
        recv_sem.at[5],
    )
    settle(r5, recv_sem.at[5])

    ahead, behind = lax.rem(flow + 1, FLOW), lax.rem(flow + FLOW - 1, FLOW)
    above, below = lax.rem(cy + 1, CY), lax.rem(cy + CY - 1, CY)
    copies = []

    def halo(n, source, target, device):
        copies.append(
            pltpu.make_async_remote_copy(
                src_ref=source,
                dst_ref=target,
                send_sem=hsend_sem.at[n],
                recv_sem=hrecv_sem.at[n],
                device_id=device,
                device_id_type=MESH,
            )
        )
        copies[-1].start()

    halo(0, r5.at[pl.ds(240, 16), :], xh.at[pl.ds(0, 16), :], {"flow": ahead})
    halo(1, r5.at[pl.ds(0, 16), :], xh.at[pl.ds(16, 16), :], {"flow": behind})
    ys[0:16, :] = r5[pl.ds(15, 16, stride=16), :]
    ys[16:32, :] = r5[pl.ds(0, 16, stride=16), :]
    halo(2, ys.at[pl.ds(0, 16), :], yh.at[pl.ds(0, 16), :], {"cy": above})
    halo(3, ys.at[pl.ds(16, 16), :], yh.at[pl.ds(16, 16), :], {"cy": below})
    packed = [jnp.zeros((16, 128), f32), jnp.zeros((16, 128), f32)]
    lane = lax.broadcasted_iota(jnp.int32, (16, 128), 1)
    for x in range(16):
        at = 16 * (x // 2)
        moved = pltpu.roll(r5[16 * x : 16 * x + 16, :], (at + 1) % 128, 1)
        packed[x % 2] = jnp.where((lane == at) | (lane == at + 1), moved, packed[x % 2])
    zs[0:16, :] = packed[0]
    zs[16:32, :] = packed[1]
    halo(4, zs, zh, {"cz": 1 - cz})
    for copy in copies:
        copy.wait()
    fill_fields(r5, xh, yh, zh, field)
    finish(pops, aux, field, post)
    stores = [
        pltpu.make_async_copy(post, post_out, store_sem.at[0]),
        pltpu.make_async_copy(r5, phi_out, store_sem.at[1]),
    ]
    for copy in stores:
        copy.start()
    gather_faces(post, xf, yf, zf, corner)
    copies = []
    for n, (source, target, i, j, k) in enumerate(messages):
        copies.append(
            pltpu.make_async_remote_copy(
                src_ref=source,
                dst_ref=target,
                send_sem=fsend_sem.at[n],
                recv_sem=frecv_sem.at[n],
                device_id=partner(i, j, k),
                device_id_type=MESH,
            )
        )
        copies[-1].start()
    for n, ref in enumerate((s0, s1, s2, s3, s4, s5)):
        if n in (1, 4):
            settle(ref.at[:, pl.ds(0, 120), :], send_sem.at[n])
        else:
            settle(ref.at[pl.ds(0, 240), :], send_sem.at[n])


    for copy in copies:
        copy.wait()
    for n, (out, got) in enumerate(
        ((xo, xr), (yo, yr), (zo, zr), (zxo, zx), (zyo, zy), (co, cr))
    ):
        stores.append(pltpu.make_async_copy(got, out, store_sem.at[2 + n]))
        stores[-1].start()
    for copy in stores:
        copy.wait()


def collide_all(table, flow_pops, ion_pos, ion_neg, gray):
    rows = (256, 128)
    halves = (2, 128, 128)
    anywhere = pl.BlockSpec(memory_space=pl.ANY)
    shapes = [(33, 256, 128), rows, *FACE_SHAPES]
    buffers = [(256, 256), (128, 128), (256, 256), (NX + NY + 8, 128), (7, 256, 128), (3, 256, 128)]
    buffers += [rows, rows, halves, halves, rows, rows, rows, rows, halves, halves, rows, rows]
    buffers += [(32, 128)] * 5
    buffers += [(14, 16, 128), (14, 16, 128), (32, 128), (4, 8, 128)] + FACE_SHAPES
    return pl.pallas_call(
        main_kernel,
        out_shape=[jax.ShapeDtypeStruct(s, f32) for s in shapes],
        in_specs=[pl.BlockSpec(memory_space=pltpu.SMEM)] + [anywhere] * 8,
        out_specs=[anywhere] * 8,
        scratch_shapes=[pltpu.VMEM((33, 256, 128), f32)] * 2
        + [pltpu.VMEM(rows, jnp.int32)]
        + [pltpu.VMEM(s, f32) for s in buffers]
        + [pltpu.SemaphoreType.DMA((n,)) for n in (8, 6, 6, 5, 5, 13, 13, 8)],
        compiler_params=pltpu.CompilerParams(
            collective_id=0, has_side_effects=True, vmem_limit_bytes=VMEM_LIMIT
        ),
        name="collision",
    )(table, ion_pos, ion_neg, flow_pops, gray, *(jnp.asarray(t) for t in tables()))


def run_population(q, load, xr, yr, zr, zx, zy, cr, store):
    ex, ey, ez = DIRS[q]
    lane = lax.broadcasted_iota(jnp.int32, (16, 128), 1)
    row = lax.broadcasted_iota(jnp.int32, (16, 128), 0)
    last_row, first_row = (15, 0) if ey == 1 else (0, 15)
    for x in range(16):
        xs = x - ex
        outside = xs < 0 or xs > 15
        if outside:
            plane = xr[FACE[0, ex].index(q) + (0 if ex == 1 else 7)]
        else:
            plane = load(xs)
        if ey:
            if outside:
                n = {7: 0, 8: 1, 9: 2, 10: 3}[q]
                tile = 7 if ey == 1 else 0
                line = cr[n, tile : tile + 1, :]
            else:
                line = yr[FACE[1, ey].index(q) + (0 if ey == 1 else 7), xs : xs + 1, :]
            plane = jnp.where(row == first_row, line, pltpu.roll(plane, ey % 16, 0))
        if ez:
            face = FACE[2, ez].index(q)
            if outside:
                edge = zx[0:16, :] if ex == 1 else zx[16:32, :]
                block = 7 if ex == 1 else 0
            else:
                edge = zr[16 * (xs % 2) : 16 * (xs % 2) + 16, :]
                block = xs // 2
            at = 16 * block + 2 * face + (0 if ez == 1 else 1)
            if ey:
                beyond = zy[0 if ey == 1 else 1, 16 * (xs % 2) : 16 * (xs % 2) + 16, :]
                edge = pltpu.roll(jnp.where(row == last_row, beyond, edge), ey % 16, 0)
            goal = 0 if ez == 1 else 127
            moved = pltpu.roll(edge, (goal - at) % 128, 1) if (goal - at) % 128 else edge
            plane = jnp.where(lane == goal, moved, pltpu.roll(plane, ez % 128, 1))
        store(x, plane)


def running_kernel(
    post_hbm, phi_hbm, x_hbm, y_hbm, z_hbm, zx_hbm, zy_hbm, c_hbm,
    flow_out, pos_out, neg_out, phi_out,
    post, moved, xr, yr, zr, zx, zy, cr, in_sem, out_sem, face_sem,
):
    def output(q):
        if q < 19:
            return flow_out.at[q]
        return pos_out.at[q - 19] if q < 26 else neg_out.at[q - 26]

    pairs = ((x_hbm, xr), (y_hbm, yr), (z_hbm, zr), (zx_hbm, zx), (zy_hbm, zy), (c_hbm, cr))
    faces = [pltpu.make_async_copy(a, b, face_sem.at[n]) for n, (a, b) in enumerate(pairs)]
    reads = [pltpu.make_async_copy(post_hbm.at[q], post.at[q], in_sem.at[q]) for q in range(33)]
    writes = []
    for q in range(33):
        source = post if DIRS[q] == (0, 0, 0) else moved
        writes.append(pltpu.make_async_copy(source.at[q], output(q), out_sem.at[q]))
    writes.append(pltpu.make_async_copy(phi_hbm, phi_out, out_sem.at[33]))
    for copy in (reads[0], *faces, *reads[1:], writes[33]):
        copy.start()
    for q in range(33):
        reads[q].wait()
        if q == 1:
            for copy in faces:
                copy.wait()
        if DIRS[q] != (0, 0, 0):

            def load(x, q=q):
                return post[q, 16 * x : 16 * x + 16, :]

            def store(x, plane, q=q):
                moved[q, 16 * x : 16 * x + 16, :] = plane

            run_population(q, load, xr, yr, zr, zx, zy, cr, store)
        writes[q].start()
    for copy in writes:
        copy.wait()


def run_all(post, phi, faces):
    anywhere = pl.BlockSpec(memory_space=pl.ANY)
    shapes = [(19, 256, 128), (7, 256, 128), (7, 256, 128), (256, 128)]
    return pl.pallas_call(
        running_kernel,
        out_shape=[jax.ShapeDtypeStruct(s, f32) for s in shapes],
        in_specs=[anywhere] * 8,
        out_specs=[anywhere] * 4,
        scratch_shapes=[pltpu.VMEM((33, 256, 128), f32)] * 2
        + [pltpu.VMEM(s, f32) for s in FACE_SHAPES]
        + [pltpu.SemaphoreType.DMA((n,)) for n in (33, 34, 6)],
        compiler_params=pltpu.CompilerParams(vmem_limit_bytes=VMEM_LIMIT),
        name="running",
    )(post, phi, *faces)


def shards(flow_pops, ion_pos, ion_neg, gray_class, fraction_table):
    extent = gray_class.shape
    flow_pops = flow_pops.reshape(19, 256, 128)
    ion_pos = ion_pos.reshape(7, 256, 128)
    ion_neg = ion_neg.reshape(7, 256, 128)
    gray = gray_class.reshape(256, 128)
    post, phi, *faces = collide_all(fraction_table, flow_pops, ion_pos, ion_neg, gray)
    flow_new, pos_new, neg_new, phi = run_all(post, phi, faces)
    return (
        flow_new.reshape(19, *extent),
        pos_new.reshape(7, *extent),
        neg_new.reshape(7, *extent),
        phi.reshape(extent),
    )


def solution(mesh):
    in_specs = (
        P(None, "flow", "cy", "cz"),
        P(None, "flow", "cy", "cz"),
        P(None, "flow", "cy", "cz"),
        P("flow", "cy", "cz"),
        P(),
    )
    out_specs = (
        P(None, "flow", "cy", "cz"),
        P(None, "flow", "cy", "cz"),
        P(None, "flow", "cy", "cz"),
        P("flow", "cy", "cz"),
    )
    return jax.shard_map(shards, mesh=mesh, in_specs=in_specs, out_specs=out_specs, check_vma=False)
```

time: 81.8 us -> 68.3 us (0.83)
  local copies, waits for them, and re-layouts: 6.69 us -> 0 us
  Pallas kernels: 74.1 us -> 67.5 us
    unnamed x19 -> x0, local copies, waits for them, and re-layouts: 6.69 us -> none
    pallas_call x4 -> x2, Pallas kernels: 74.1 us -> 67.5 us  [the longest x1 61.8 us: collide_all(): pl.pallas_call(main_kernel, out_shape=[jax.ShapeDtypeStruct(s, f32) for s...]
where the time goes in v1:
time: 68.3 us; the launch traced here: 68.2 us
  Pallas kernels  67.5 us (99%)
    pallas_call x1, Pallas kernels, collide_all(): pl.pallas_call(main_kernel, out_shape=[jax.ShapeDtypeStruct(s, f32) for s...  61.8 us
    pallas_call x1, Pallas kernels, run_all(): pl.pallas_call(running_kernel, out_shape=[jax.ShapeDtypeStruct(s, f32) fo...  5.78 us

profile of v1, /device:TPU:1, one launch (start us, length us, event | category | flops | bytes accessed | tf_op | source)
XLA Modules:
  0.0 68.2 jit_solution(9390117538737626903)
XLA Ops:
  0.6 61.8 %collision.1 = (f32[33,256,128]{2,1,0:T(8,128)}, f32[256,128]{1,0:T(8,128)}, f32[14,16,128]{2,1,0:T(8,128)}, f32[14,16,128]{2,1,0:T(8,128)}, f32[32,128]{1,0:T(8...) custom-call(f32[16]{0:T(128)} %table_ref.1, f32[7,256,128]{2,1,0:T(8,128)} %bitcast.9, ...), custom_call_target="tpu_custom_call" | custom-call | tf_op jit(solution)/shard_map/collision/pallas_call | solution.py:511
  62.4 5.8 %running.1 = (f32[19,256,128]{2,1,0:T(8,128)}, f32[7,256,128]{2,1,0:T(8,128)}, f32[7,256,128]{2,1,0:T(8,128)}, f32[256,128]{1,0:T(8,128)}) custom-call(f32[33,256,128]{2,1,0:T(8,128)} %get-tuple-element.16.post_hbm, f32[256,128]{1,0:T(8,128)} %get-tuple-element.17.phi_hbm, f32[14,16,128]{2,1,0:T(8,128)} %get-tuple-element.18.x_hbm, ...), custom_call_target="tpu_custom_call" | custom-call | tf_op jit(solution)/shard_map/running/pallas_call | solution.py:607

commit v2 on v1

--- a/solution.py
+++ b/solution.py
@@ -50,26 +50,51 @@
 }
 
 
-def cas_table(points_k, points_n, length):
+def cas_table64(points_k, points_n, length):
     product = (points_k[:, None].astype(np.int64) * points_n[None, :]) % length
     angle = product * (2.0 * math.pi / length)
-    return (np.cos(angle) + np.sin(angle)).astype(np.float32)
+    return np.cos(angle) + np.sin(angle)
+
+
+def cas_table(points_k, points_n, length):
+    return cas_table64(points_k, points_n, length).astype(np.float32)
 
 
 def tables():
-    order = np.array([16 * a + b for b in range(16) for a in range(16)])
-    hx = cas_table(order, order, NX)
     hy = cas_table(np.arange(NY), np.arange(NY), NY)
-    hz = cas_table(np.arange(NZ), np.arange(NZ), NZ)
-
-    def lam(modes, length):
-        return 4.0 * np.sin(np.pi * modes / length) ** 2
-
-    rows = np.zeros((NX + NY + 8, 128))
-    rows[:NX] = lam(order, NX)[:, None]
-    rows[NX : NX + NY] = lam(np.arange(NY), NY)[:, None]
-    rows[NX + NY : NX + NY + 2] = lam(np.arange(NZ), NZ).reshape(2, 128)
-    return hx, hy, hz, rows.astype(np.float32)
+    z = np.arange(NZ)
+    hz = cas_table(z, z, NZ)
+    wide = cas_table64(z, z, NZ)
+    slope = -0.5 * (np.roll(wide, -1, 1) - np.roll(wide, 1, 1))
+    back = [
+        np.concatenate([wide[:, 128 * c : 128 * c + 128], slope[:, 128 * c : 128 * c + 128]], 1)
+        for c in range(CZ)
+    ]
+    lam_y = 4.0 * np.sin(np.pi * np.arange(NY) / NY) ** 2
+    lam_z = 4.0 * np.sin(np.pi * z / NZ) ** 2
+    t = 1.0 + 0.5 * (lam_y[:, None] + lam_z[None, :])
+    mu = 1.0 / (t + np.sqrt(t * t - 1.0))
+    gap = 1.0 / mu - mu
+    gap[0, 0] = 1.0
+    scale = coupling / (NY * NZ) / gap
+    mu[0, 0] = scale[0, 0] = 0.0
+    window = np.arange(128) // 16
+    per_rank = []
+    for b in range(16):
+        m = np.tile(mu[:, 16 * b : 16 * b + 16], (1, 8))
+        c = np.tile(scale[:, 16 * b : 16 * b + 16], (1, 8))
+        packed = mu[:, 16 * b : 16 * b + 16].reshape(2, 8, 8, 16).transpose(0, 2, 1, 3).reshape(16, 128)
+        per_rank.append(
+            np.concatenate(
+                [m, m ** (window + 1), m ** (8 - window), m**8, c, packed**16, 1.0 / (1.0 - packed**256)]
+            )
+        )
+    return (
+        np.concatenate([hy, hy], 1),
+        hz.reshape(CZ, 128, NZ),
+        np.stack(back).astype(np.float32),
+        np.stack(per_rank).astype(np.float32),
+    )
 
 
 def place():
@@ -95,20 +120,18 @@
 def swap_across_plane(source, target, send_sem, recv_sem):
     _, cy, cz = place()
     me = cz * CY + cy
-
-    def step(k, carry):
-        other = lax.rem(me + k, 16)
-        pltpu.make_async_remote_copy(
-            src_ref=source(other),
-            dst_ref=target(me),
-            send_sem=send_sem,
-            recv_sem=recv_sem,
-            device_id={"cy": lax.rem(other, CY), "cz": lax.div(other, CY)},
-            device_id_type=MESH,
-        ).start()
-        return carry
-
-    lax.fori_loop(1, 16, step, 0)
+    for step_cy in (4, 5, 3, 2, 6, 7, 1, 0):
+        for step_cz in (1, 0):
+            if step_cy or step_cz:
+                to_cy, to_cz = lax.rem(cy + step_cy, CY), lax.rem(cz + step_cz, CZ)
+                pltpu.make_async_remote_copy(
+                    src_ref=source(to_cz * CY + to_cy),
+                    dst_ref=target(me),
+                    send_sem=send_sem,
+                    recv_sem=recv_sem,
+                    device_id={"cy": to_cy, "cz": to_cz},
+                    device_id_type=MESH,
+                ).start()
     pltpu.make_async_copy(source(me), target(me), recv_sem).start()
 
 
@@ -135,8 +158,151 @@
     return ref.at[pl.ds(pl.multiple_of(start, count), count), :]
 
 
-def halves_at(ref, start, count):
-    return ref.at[:, pl.ds(pl.multiple_of(start, count), count), :]
+def window_of(shape):
+    return lax.broadcasted_iota(jnp.int32, shape, 1) // 16
+
+
+def swap_windows(blocks):
+    window = window_of(blocks[0].shape)
+    for s in (1, 2, 4):
+        high = (window & s) != 0
+        moved = list(blocks)
+        for i in range(8):
+            if not i & s:
+                low_block, high_block = blocks[i], blocks[i + s]
+                moved[i] = jnp.where(high, pltpu.roll(high_block, 16 * s, 1), low_block)
+                moved[i + s] = jnp.where(high, high_block, pltpu.roll(low_block, 128 - 16 * s, 1))
+        blocks = moved
+    return blocks
+
+
+def spread(values, j):
+    values = jnp.where(window_of(values.shape) == j, values, 0.0)
+    for s in (16, 32, 64):
+        values = values + pltpu.roll(values, s, 1)
+    return values
+
+
+def pack_windows(values, j):
+    window = window_of((8, 128))
+    packed = []
+    for half in range(2):
+        both = jnp.zeros((8, 128), f32)
+        for i in range(8):
+            tile = values[64 * half + 8 * i : 64 * half + 8 * i + 8, :]
+            shift = (16 * (i - j)) % 128
+            both = jnp.where(window == i, pltpu.roll(tile, shift, 1) if shift else tile, both)
+        packed.append(both)
+    return jnp.concatenate(packed, axis=0)
+
+
+def scan_up(values, factor):
+    window = window_of(values.shape)
+    for s in (1, 2, 4):
+        moved = pltpu.roll(values, 16 * s, 1)
+        if factor is not None:
+            moved = factor * moved
+            factor = factor * factor
+        values = values + jnp.where(window >= s, moved, 0.0)
+    return values
+
+
+def scan_down(values, factor):
+    window = window_of(values.shape)
+    for s in (1, 2, 4):
+        moved = factor * pltpu.roll(values, 128 - 16 * s, 1)
+        factor = factor * factor
+        values = values + jnp.where(window < 8 - s, moved, 0.0)
+    return values
+
+
+def total_of(values):
+    return jnp.sum(jnp.sum(values, axis=0, keepdims=True), axis=1, keepdims=True)
+
+
+def zero_mode_mask(cy, cz):
+    row = lax.broadcasted_iota(jnp.int32, (8, 128), 0)
+    lane = lax.broadcasted_iota(jnp.int32, (8, 128), 1)
+    here = jnp.where(cy + cz == 0, 1.0, 0.0)
+    return jnp.where((row == 0) & (lane % 16 == 0), here, 0.0)
+
+
+def block_moments(rho, gtab, moments, partial, mask):
+    mu, near, far, eighth = (gtab[128 * n : 128 * n + 128, :] for n in range(4))
+    up = [scan_up(r, mu) for r in rho]
+    down = [scan_down(r, mu) for r in rho]
+    moments[0:16, :] = pack_windows(up[1] + eighth * up[0], 7)
+    moments[16:32, :] = pack_windows(down[0] + eighth * down[1], 0)
+    window = window_of((8, 128)).astype(f32)
+    at = (window - 7.5, window + 0.5)
+    zero = [rho[g][0:8, :] * mask for g in range(2)]
+    row = lax.broadcasted_iota(jnp.int32, (8, 128), 0)
+    tile = jnp.zeros((8, 128), f32)
+    for n in range(3):
+        weighted = zero[0] * at[0] ** n + zero[1] * at[1] ** n if n else zero[0] + zero[1]
+        tile = jnp.where(row == n, total_of(weighted), tile)
+    moments[32:40, :] = tile
+
+    def rest():
+        partial[0] = up[0] + (down[0] - rho[0]) + far * spread(down[1], 0)
+        partial[1] = up[1] + (down[1] - rho[1]) + near * spread(up[0], 7)
+
+    return rest
+
+
+def gathered_potential(rho_first, gtab, gathered, partial, mask, flow, out):
+    def packed(source, start):
+        return gathered[pl.ds(pl.multiple_of(40 * source + start, 8), 16), :]
+
+    ratio, image = gtab[640:656, :], gtab[656:672, :]
+    left, right = packed(flow, 0), packed(flow, 16)
+    for d in range(15, 0, -1):
+        left = packed(lax.rem(flow + 16 - d, 16), 0) + ratio * left
+        right = packed(lax.rem(flow + d, 16), 16) + ratio * right
+    left, right = left * image, right * image
+    for tile in range(16):
+        rows = slice(8 * tile, 8 * tile + 8)
+        half = 8 * (tile // 8)
+        from_left = spread(left[half : half + 8, :], tile % 8)
+        from_right = spread(right[half : half + 8, :], tile % 8)
+        near, far, eighth, scale = (
+            gtab[128 * n + 8 * tile : 128 * n + 8 * tile + 8, :] for n in range(1, 5)
+        )
+        out[rows, 0:128] = scale * (
+            partial[0, rows, :] + near * from_left + (far * eighth) * from_right
+        )
+        out[rows, 128:256] = scale * (
+            partial[1, rows, :] + (near * eighth) * from_left + far * from_right
+        )
+
+    def moment(block, n):
+        return gathered[40 * block + 32 + n : 40 * block + 33 + n, :]
+
+    mean = sum((moment(n, 0) for n in range(1, 16)), moment(0, 0)) * (1.0 / NX)
+    first = second = left_sum = left_first = jnp.zeros((1, 128), f32)
+    for block in range(16):
+        centre = 16.0 * block - 120.0
+        own = moment(block, 0) - 16.0 * mean
+        own_first = centre * own + moment(block, 1)
+        first = first + own_first
+        second = second + (centre * own_first + centre * moment(block, 1))
+        second = second + (moment(block, 2) - 340.0 * mean)
+        before = jnp.where(block < flow, 1.0, 0.0)
+        left_sum = left_sum + before * own
+        left_first = left_first + before * own_first
+    window = window_of((8, 128)).astype(f32)
+    centre = 16.0 * flow.astype(f32) - 120.0
+    for g in range(2):
+        at = centre + (window - 7.5 + 8.0 * g)
+        zero = (rho_first[g] - mean) * mask
+        to_here, to_here_first = scan_up(zero, None), scan_up(zero * at, None)
+        upto, upto_first = left_sum + to_here, left_first + to_here_first
+        left_sum = left_sum + spread(to_here, 7)
+        left_first = left_first + spread(to_here_first, 7)
+        distance = 2.0 * (at * upto - upto_first) + first
+        value = (second - 2.0 * at * first) * (0.5 / NX) - 0.5 * distance
+        lanes = slice(128 * g, 128 * g + 128)
+        out[0:8, lanes] = out[0:8, lanes] + (coupling / (NY * NZ)) * (mask * value)
 
 
 def pick_solid(gray, table_ref):
@@ -150,8 +316,7 @@
     return values[0]
 
 
-def fill_fields(phi, xh, yh, zh, field):
-    lane = lax.broadcasted_iota(jnp.int32, (16, 128), 1)
+def fill_fields(phi, xh, yh, field):
     row = lax.broadcasted_iota(jnp.int32, (16, 128), 0)
     for x in range(16):
         here = phi[16 * x : 16 * x + 16, :]
@@ -161,13 +326,6 @@
         low = jnp.where(row == 0, yh[x : x + 1, :], pltpu.roll(here, 1, 0))
         high = jnp.where(row == 15, yh[16 + x : 17 + x, :], pltpu.roll(here, 15, 0))
         field[1, 16 * x : 16 * x + 16, :] = -0.5 * (high - low)
-        edge = zh[16 * (x % 2) : 16 * (x % 2) + 16, :]
-        at = 16 * (x // 2)
-        low = jnp.where(lane == 0, pltpu.roll(edge, (128 - at) % 128, 1), pltpu.roll(here, 1, 1))
-        high = jnp.where(
-            lane == 127, pltpu.roll(edge, (127 - at - 1) % 128, 1), pltpu.roll(here, 127, 1)
-        )
-        field[2, 16 * x : 16 * x + 16, :] = -0.5 * (high - low)
 
 
 def prepare(pops, charge, gray, table_ref, aux):
@@ -300,33 +458,33 @@
 
 
 def main_kernel(
-    table_ref, pos_hbm, neg_hbm, flow_hbm, gray_hbm, hx_hbm, hy_hbm, hz_hbm, lam_hbm,
+    table_ref, pos_hbm, neg_hbm, flow_hbm, gray_hbm, hy_hbm, hz_hbm, back_hbm, gtab_hbm,
     post_out, phi_out, xo, yo, zo, zxo, zyo, co,
-    pops, post, gray, hx_ref, hy_ref, hz_ref, lam_ref, aux, field,
-    s0, r0, s1, r1, s2, r2, s3, r3, s4, r4, s5, r5, ys, zs, xh, yh, zh,
+    pops, post, gray, hy_ref, hz_ref, back_ref, gtab, aux, field, charge,
+    s0, r0, moments, gathered, partial, modes, s1, r1, joined, phi, ys, xh, yh,
     xf, yf, zf, corner, xr, yr, zr, zx, zy, cr,
     load_sem, send_sem, recv_sem, hsend_sem, hrecv_sem, fsend_sem, frecv_sem, store_sem,
 ):
     flow, cy, cz = place()
+    me = cz * CY + cy
     loads = [
         pltpu.make_async_copy(source, target, load_sem.at[n])
         for n, (source, target) in enumerate(
             (
                 (pos_hbm, pops.at[pl.ds(19, 7)]),
                 (neg_hbm, pops.at[pl.ds(26, 7)]),
-                (hy_hbm, hy_ref),
-                (hz_hbm, hz_ref),
+                (hz_hbm.at[cz], hz_ref),
                 (flow_hbm, pops.at[pl.ds(0, 19)]),
                 (gray_hbm, gray),
-                (hx_hbm, hx_ref),
-                (lam_hbm, lam_ref),
+                (hy_hbm, hy_ref),
+                (gtab_hbm.at[me], gtab),
+                (back_hbm.at[cz], back_ref),
             )
         )
     ]
     for copy in loads:
         copy.start()
     barrier = pltpu.get_barrier_semaphore()
-    me = cz * CY + cy
 
     def greet(k, carry):
         other = lax.rem(me + k, 16)
@@ -346,84 +504,71 @@
     strangers = [m[2:] for m in messages if m[2] and (m[3] or m[4])]
     for i, j, k in strangers:
         pl.semaphore_signal(barrier, inc=1, device_id=partner(i, j, k), device_id_type=MESH)
-    loads[0].wait()
-    loads[1].wait()
+    for copy in loads[:3]:
+        copy.wait()
     pos = pops[19]
     neg = pops[26]
     for q in range(1, 7):
         pos = pos + pops[19 + q]
         neg = neg + pops[26 + q]
-    s0[...] = pos - neg
+    charge[...] = pos - neg
+
+    spectrum = fdot(charge[...], hz_ref[...])
+    for g in range(2):
+        for c in range(2):
+            blocks = [
+                spectrum[128 * g + 16 * i : 128 * g + 16 * i + 16, 128 * c : 128 * c + 128]
+                for i in range(8)
+            ]
+            for i, block in enumerate(swap_windows(blocks)):
+                at = 16 * (8 * c + i)
+                s0[at : at + 16, 128 * g : 128 * g + 128] = block
     pl.semaphore_wait(barrier, 30 + len(strangers))
-
     swap_across_plane(
         lambda b: rows_at(s0, 16 * b, 16),
         lambda b: rows_at(r0, 16 * b, 16),
         send_sem.at[0],
         recv_sem.at[0],
     )
-    for copy in loads[2:]:
+    for copy in loads[3:]:
         copy.wait()
-    prepare(pops, s0, gray, table_ref, aux)
+    prepare(pops, charge, gray, table_ref, aux)
     settle(r0, recv_sem.at[0])
-    hy = hy_ref[...]
-    half = [fdot(hy, r0[128 * c : 128 * c + 128, :]) for c in range(2)]
-    spectrum = fdot(jnp.concatenate(half, axis=1), hz_ref[...])
-    s1[0] = spectrum[:, :128]
-    s1[1] = spectrum[:, 128:]
+    spectrum = fdot(hy_ref[...], r0[...])
+    rho = [spectrum[:, :128], spectrum[:, 128:]]
+    mask = zero_mode_mask(cy, cz)
+    rest = block_moments(rho, gtab, moments, partial, mask)
     swap_along_flow(
-        lambda a: halves_at(s1, 8 * a, 8),
-        lambda a: halves_at(r1, 8 * a, 8),
+        lambda a: moments,
+        lambda a: gathered.at[pl.ds(pl.multiple_of(40 * a, 8), 40), :],
         send_sem.at[1],
         recv_sem.at[1],
     )
-    settle(r1, recv_sem.at[1])
-    for b in range(16):
-        s2[16 * b : 16 * b + 16, :] = r1[b // CY, pl.ds(b % CY, 16, stride=8), :]
+    rest()
+    settle(gathered, recv_sem.at[1])
+    gathered_potential(
+        [r[0:8, :] for r in rho], gtab, gathered, partial, mask, flow, modes
+    )
+    s1[...] = fdot(hy_ref[:, 0:128], modes[...])
     swap_across_plane(
-        lambda b: rows_at(s2, 16 * b, 16),
-        lambda b: rows_at(r2, 16 * b, 16),
+        lambda b: rows_at(s1, 16 * lax.rem(b, CY), 16),
+        lambda b: rows_at(r1, 16 * b, 16),
         send_sem.at[2],
         recv_sem.at[2],
     )
-    total = (
-        lam_ref[0:NX, :]
-        + lam_ref[pl.ds(NX + CY * flow + cy, 1), :]
-        + lam_ref[pl.ds(NX + NY + cz, 1), :]
-    )
-    scale = coupling / (NX * NY * NZ)
-    green = jnp.where(total > 0.0, scale / jnp.where(total > 0.0, total, 1.0), 0.0)
-    settle(r2, recv_sem.at[2])
-    modes = green * fdot(hx_ref[...], r2[...])
-    s3[...] = fdot(hx_ref[...], modes)
-    swap_across_plane(
-        lambda b: rows_at(s3, 16 * b, 16),
-        lambda b: rows_at(r3, 16 * b, 16),
-        send_sem.at[3],
-        recv_sem.at[3],
-    )
-    settle(r3, recv_sem.at[3])
-    for a in range(16):
+    settle(r1, recv_sem.at[2])
+    for g in range(2):
         for c in range(2):
-            s4[c, 8 * a : 8 * a + 8, :] = r3[pl.ds(128 * c + a, 8, stride=16), :]
-    swap_along_flow(
-        lambda a: halves_at(s4, 8 * a, 8),
-        lambda a: halves_at(r4, 8 * a, 8),
-        send_sem.at[4],
-        recv_sem.at[4],
-    )
-    settle(r4, recv_sem.at[4])
-    half = [fdot(hy, r4[c]) for c in range(2)]
-    plane = fdot(jnp.concatenate(half, axis=1), hz_ref[...])
-    s5[0:128, :] = plane[:, :128]
-    s5[128:256, :] = plane[:, 128:]
-    swap_across_plane(
-        lambda b: rows_at(s5, 16 * b, 16),
-        lambda b: rows_at(r5, 16 * b, 16),
-        send_sem.at[5],
-        recv_sem.at[5],
-    )
-    settle(r5, recv_sem.at[5])
+            blocks = [
+                r1[128 * c + 16 * i : 128 * c + 16 * i + 16, 128 * g : 128 * g + 128]
+                for i in range(8)
+            ]
+            for i, block in enumerate(swap_windows(blocks)):
+                at = 128 * g + 16 * i
+                joined[at : at + 16, 128 * c : 128 * c + 128] = block
+    both = fdot(joined[...], back_ref[...])
+    phi[...] = both[:, :128]
+    field[2] = both[:, 128:]
 
     ahead, behind = lax.rem(flow + 1, FLOW), lax.rem(flow + FLOW - 1, FLOW)
     above, below = lax.rem(cy + 1, CY), lax.rem(cy + CY - 1, CY)
@@ -442,28 +587,19 @@
         )
         copies[-1].start()
 
-    halo(0, r5.at[pl.ds(240, 16), :], xh.at[pl.ds(0, 16), :], {"flow": ahead})
-    halo(1, r5.at[pl.ds(0, 16), :], xh.at[pl.ds(16, 16), :], {"flow": behind})
-    ys[0:16, :] = r5[pl.ds(15, 16, stride=16), :]
-    ys[16:32, :] = r5[pl.ds(0, 16, stride=16), :]
+    halo(0, phi.at[pl.ds(240, 16), :], xh.at[pl.ds(0, 16), :], {"flow": ahead})
+    halo(1, phi.at[pl.ds(0, 16), :], xh.at[pl.ds(16, 16), :], {"flow": behind})
+    ys[0:16, :] = phi[pl.ds(15, 16, stride=16), :]
+    ys[16:32, :] = phi[pl.ds(0, 16, stride=16), :]
     halo(2, ys.at[pl.ds(0, 16), :], yh.at[pl.ds(0, 16), :], {"cy": above})
     halo(3, ys.at[pl.ds(16, 16), :], yh.at[pl.ds(16, 16), :], {"cy": below})
-    packed = [jnp.zeros((16, 128), f32), jnp.zeros((16, 128), f32)]
-    lane = lax.broadcasted_iota(jnp.int32, (16, 128), 1)
-    for x in range(16):
-        at = 16 * (x // 2)
-        moved = pltpu.roll(r5[16 * x : 16 * x + 16, :], (at + 1) % 128, 1)
-        packed[x % 2] = jnp.where((lane == at) | (lane == at + 1), moved, packed[x % 2])
-    zs[0:16, :] = packed[0]
-    zs[16:32, :] = packed[1]
-    halo(4, zs, zh, {"cz": 1 - cz})
     for copy in copies:
         copy.wait()
-    fill_fields(r5, xh, yh, zh, field)
+    fill_fields(phi, xh, yh, field)
     finish(pops, aux, field, post)
     stores = [
         pltpu.make_async_copy(post, post_out, store_sem.at[0]),
-        pltpu.make_async_copy(r5, phi_out, store_sem.at[1]),
+        pltpu.make_async_copy(phi, phi_out, store_sem.at[1]),
     ]
     for copy in stores:
         copy.start()
@@ -481,13 +617,9 @@
             )
         )
         copies[-1].start()
-    for n, ref in enumerate((s0, s1, s2, s3, s4, s5)):
-        if n in (1, 4):
-            settle(ref.at[:, pl.ds(0, 120), :], send_sem.at[n])
-        else:
-            settle(ref.at[pl.ds(0, 240), :], send_sem.at[n])
-
-
+    settle(s0.at[pl.ds(0, 240), :], send_sem.at[0])
+    settle(gathered.at[pl.ds(0, 600), :], send_sem.at[1])
+    settle(s0.at[pl.ds(0, 240), :], send_sem.at[2])
     for copy in copies:
         copy.wait()
     for n, (out, got) in enumerate(
@@ -500,13 +632,12 @@
 
 
 def collide_all(table, flow_pops, ion_pos, ion_neg, gray):
-    rows = (256, 128)
-    halves = (2, 128, 128)
+    rows, square = (256, 128), (256, 256)
     anywhere = pl.BlockSpec(memory_space=pl.ANY)
     shapes = [(33, 256, 128), rows, *FACE_SHAPES]
-    buffers = [(256, 256), (128, 128), (256, 256), (NX + NY + 8, 128), (7, 256, 128), (3, 256, 128)]
-    buffers += [rows, rows, halves, halves, rows, rows, rows, rows, halves, halves, rows, rows]
-    buffers += [(32, 128)] * 5
+    buffers = [(128, 256), (128, 256), square, (672, 128), (7, 256, 128), (3, 256, 128), rows]
+    buffers += [square, square, (40, 128), (640, 128), (2, 128, 128), (128, 256), (128, 256), square, square]
+    buffers += [rows, (32, 128), (32, 128), (32, 128)]
     buffers += [(14, 16, 128), (14, 16, 128), (32, 128), (4, 8, 128)] + FACE_SHAPES
     return pl.pallas_call(
         main_kernel,
@@ -516,7 +647,7 @@
         scratch_shapes=[pltpu.VMEM((33, 256, 128), f32)] * 2
         + [pltpu.VMEM(rows, jnp.int32)]
         + [pltpu.VMEM(s, f32) for s in buffers]
-        + [pltpu.SemaphoreType.DMA((n,)) for n in (8, 6, 6, 5, 5, 13, 13, 8)],
+        + [pltpu.SemaphoreType.DMA((n,)) for n in (8, 3, 3, 4, 4, 13, 13, 8)],
         compiler_params=pltpu.CompilerParams(
             collective_id=0, has_side_effects=True, vmem_limit_bytes=VMEM_LIMIT
         ),

time: 68.3 us -> 55.2 us (0.81)
  Pallas kernels: 67.5 us -> 54.5 us
    pallas_call x1, Pallas kernels: 61.8 us -> 48.7 us  [collide_all(): pl.pallas_call(main_kernel, out_shape=[jax.ShapeDtypeStruct(s, f32) for s...]
where the time goes in v2:
time: 55.2 us; the launch traced here: 55.1 us
  Pallas kernels  54.5 us (99%)
  between operations  0.64 us (1%)
    pallas_call x1, Pallas kernels, collide_all(): pl.pallas_call(main_kernel, out_shape=[jax.ShapeDtypeStruct(s, f32) for s...  48.7 us
    pallas_call x1, Pallas kernels, run_all(): pl.pallas_call(running_kernel, out_shape=[jax.ShapeDtypeStruct(s, f32) fo...  5.78 us

profile of v2, /device:TPU:1, one launch (start us, length us, event | category | flops | bytes accessed | tf_op | source)
XLA Modules:
  0.0 55.1 jit_solution(14976501552855884870)
XLA Ops:
  0.6 48.7 %collision.1 = (f32[33,256,128]{2,1,0:T(8,128)}, f32[256,128]{1,0:T(8,128)}, f32[14,16,128]{2,1,0:T(8,128)}, f32[14,16,128]{2,1,0:T(8,128)}, f32[32,128]{1,0:T(8...) custom-call(f32[16]{0:T(128)} %table_ref.1, f32[7,256,128]{2,1,0:T(8,128)} %bitcast.9, ...), custom_call_target="tpu_custom_call" | custom-call | tf_op jit(solution)/shard_map/collision/pallas_call | solution.py:642
  49.3 5.8 %running.1 = (f32[19,256,128]{2,1,0:T(8,128)}, f32[7,256,128]{2,1,0:T(8,128)}, f32[7,256,128]{2,1,0:T(8,128)}, f32[256,128]{1,0:T(8,128)}) custom-call(f32[33,256,128]{2,1,0:T(8,128)} %get-tuple-element.16.post_hbm, f32[256,128]{1,0:T(8,128)} %get-tuple-element.17.phi_hbm, f32[14,16,128]{2,1,0:T(8,128)} %get-tuple-element.18.x_hbm, ...), custom_call_target="tpu_custom_call" | custom-call | tf_op jit(solution)/shard_map/running/pallas_call | solution.py:738

commit v3 on v2

--- a/solution.py
+++ b/solution.py
@@ -40,7 +40,7 @@
 FLOW, CY, CZ = 16, 8, 2
 MESH = pl.DeviceIdType.MESH
 f32 = jnp.float32
-VMEM_LIMIT = 60 << 20
+VMEM_LIMIT = 55 << 20
 
 DIRS = flow_dirs + flow_dirs[:7] + flow_dirs[:7]
 FACE = {
@@ -454,16 +454,72 @@
     )
 
 
+def run_inside(post, moved):
+    for q in range(33):
+        ex, ey, ez = DIRS[q]
+        for x in range(16):
+            if 0 <= x - ex <= 15:
+                plane = post[q, 16 * (x - ex) : 16 * (x - ex) + 16, :]
+                if ey:
+                    plane = pltpu.roll(plane, ey % 16, 0)
+                if ez:
+                    plane = pltpu.roll(plane, ez % 128, 1)
+                moved[q, 16 * x : 16 * x + 16, :] = plane
+
+
+def run_edges(moved, xr, yr, zr, zx, zy, cr):
+    lane = lax.broadcasted_iota(jnp.int32, (16, 128), 1)
+    row = lax.broadcasted_iota(jnp.int32, (16, 128), 0)
+    for q in range(1, 33):
+        ex, ey, ez = DIRS[q]
+        edge_x = 0 if ex == 1 else 15
+        first_row, last_row = (0, 15) if ey == 1 else (15, 0)
+        if ex:
+            plane = xr[FACE[0, ex].index(q) + (0 if ex == 1 else 7)]
+            if ey:
+                plane = pltpu.roll(plane, ey % 16, 0)
+            if ez:
+                plane = pltpu.roll(plane, ez % 128, 1)
+            moved[q, 16 * edge_x : 16 * edge_x + 16, :] = plane
+        if ey:
+            lines = yr[FACE[1, ey].index(q) + (0 if ey == 1 else 7)]
+            if ex:
+                n = {7: 0, 8: 1, 9: 2, 10: 3}[q]
+                tile = 7 if ey == 1 else 0
+                lines = jnp.where(row == edge_x, cr[n, tile : tile + 1, :], pltpu.roll(lines, ex % 16, 0))
+            if ez:
+                lines = pltpu.roll(lines, ez % 128, 1)
+            moved[q, pl.ds(first_row, 16, stride=16), :] = lines
+        if ez:
+            face = FACE[2, ez].index(q)
+            goal = 0 if ez == 1 else 127
+            for x in range(16):
+                xs = x - ex
+                if 0 <= xs <= 15:
+                    edge = zr[16 * (xs % 2) : 16 * (xs % 2) + 16, :]
+                    block = xs // 2
+                else:
+                    edge = zx[0:16, :] if ex == 1 else zx[16:32, :]
+                    block = 7 if ex == 1 else 0
+                if ey:
+                    beyond = zy[0 if ey == 1 else 1, 16 * (xs % 2) : 16 * (xs % 2) + 16, :]
+                    edge = pltpu.roll(jnp.where(row == last_row, beyond, edge), ey % 16, 0)
+                shift = (goal - (16 * block + 2 * face + (0 if ez == 1 else 1))) % 128
+                column = pltpu.roll(edge, shift, 1) if shift else edge
+                here = slice(16 * x, 16 * x + 16)
+                moved[q, here, :] = jnp.where(lane == goal, column, moved[q, here, :])
+
+
 FACE_SHAPES = [(14, 16, 128), (14, 16, 128), (32, 128), (32, 128), (2, 32, 128), (4, 8, 128)]
 
 
 def main_kernel(
     table_ref, pos_hbm, neg_hbm, flow_hbm, gray_hbm, hy_hbm, hz_hbm, back_hbm, gtab_hbm,
-    post_out, phi_out, xo, yo, zo, zxo, zyo, co,
+    moved, phi,
     pops, post, gray, hy_ref, hz_ref, back_ref, gtab, aux, field, charge,
-    s0, r0, moments, gathered, partial, modes, s1, r1, joined, phi, ys, xh, yh,
+    s0, r0, moments, gathered, partial, modes, s1, r1, joined, ys, xh, yh,
     xf, yf, zf, corner, xr, yr, zr, zx, zy, cr,
-    load_sem, send_sem, recv_sem, hsend_sem, hrecv_sem, fsend_sem, frecv_sem, store_sem,
+    load_sem, send_sem, recv_sem, hsend_sem, hrecv_sem, fsend_sem, frecv_sem,
 ):
     flow, cy, cz = place()
     me = cz * CY + cy
@@ -597,12 +653,6 @@
         copy.wait()
     fill_fields(phi, xh, yh, field)
     finish(pops, aux, field, post)
-    stores = [
-        pltpu.make_async_copy(post, post_out, store_sem.at[0]),
-        pltpu.make_async_copy(phi, phi_out, store_sem.at[1]),
-    ]
-    for copy in stores:
-        copy.start()
     gather_faces(post, xf, yf, zf, corner)
     copies = []
     for n, (source, target, i, j, k) in enumerate(messages):
@@ -617,37 +667,32 @@
             )
         )
         copies[-1].start()
+    run_inside(post, moved)
     settle(s0.at[pl.ds(0, 240), :], send_sem.at[0])
     settle(gathered.at[pl.ds(0, 600), :], send_sem.at[1])
     settle(s0.at[pl.ds(0, 240), :], send_sem.at[2])
     for copy in copies:
         copy.wait()
-    for n, (out, got) in enumerate(
-        ((xo, xr), (yo, yr), (zo, zr), (zxo, zx), (zyo, zy), (co, cr))
-    ):
-        stores.append(pltpu.make_async_copy(got, out, store_sem.at[2 + n]))
-        stores[-1].start()
-    for copy in stores:
-        copy.wait()
+    run_edges(moved, xr, yr, zr, zx, zy, cr)
 
 
 def collide_all(table, flow_pops, ion_pos, ion_neg, gray):
     rows, square = (256, 128), (256, 256)
     anywhere = pl.BlockSpec(memory_space=pl.ANY)
-    shapes = [(33, 256, 128), rows, *FACE_SHAPES]
+    shapes = [(33, 256, 128), rows]
     buffers = [(128, 256), (128, 256), square, (672, 128), (7, 256, 128), (3, 256, 128), rows]
     buffers += [square, square, (40, 128), (640, 128), (2, 128, 128), (128, 256), (128, 256), square, square]
-    buffers += [rows, (32, 128), (32, 128), (32, 128)]
+    buffers += [(32, 128), (32, 128), (32, 128)]
     buffers += [(14, 16, 128), (14, 16, 128), (32, 128), (4, 8, 128)] + FACE_SHAPES
     return pl.pallas_call(
         main_kernel,
-        out_shape=[jax.ShapeDtypeStruct(s, f32) for s in shapes],
+        out_shape=[pltpu.VMEM(s, f32) for s in shapes],
         in_specs=[pl.BlockSpec(memory_space=pltpu.SMEM)] + [anywhere] * 8,
-        out_specs=[anywhere] * 8,
+        out_specs=[pl.BlockSpec(memory_space=pltpu.VMEM)] * 2,
         scratch_shapes=[pltpu.VMEM((33, 256, 128), f32)] * 2
         + [pltpu.VMEM(rows, jnp.int32)]
         + [pltpu.VMEM(s, f32) for s in buffers]
-        + [pltpu.SemaphoreType.DMA((n,)) for n in (8, 3, 3, 4, 4, 13, 13, 8)],
+        + [pltpu.SemaphoreType.DMA((n,)) for n in (8, 3, 3, 4, 4, 13, 13)],
         compiler_params=pltpu.CompilerParams(
             collective_id=0, has_side_effects=True, vmem_limit_bytes=VMEM_LIMIT
         ),
@@ -655,97 +700,28 @@
     )(table, ion_pos, ion_neg, flow_pops, gray, *(jnp.asarray(t) for t in tables()))
 
 
-def run_population(q, load, xr, yr, zr, zx, zy, cr, store):
-    ex, ey, ez = DIRS[q]
-    lane = lax.broadcasted_iota(jnp.int32, (16, 128), 1)
-    row = lax.broadcasted_iota(jnp.int32, (16, 128), 0)
-    last_row, first_row = (15, 0) if ey == 1 else (0, 15)
-    for x in range(16):
-        xs = x - ex
-        outside = xs < 0 or xs > 15
-        if outside:
-            plane = xr[FACE[0, ex].index(q) + (0 if ex == 1 else 7)]
-        else:
-            plane = load(xs)
-        if ey:
-            if outside:
-                n = {7: 0, 8: 1, 9: 2, 10: 3}[q]
-                tile = 7 if ey == 1 else 0
-                line = cr[n, tile : tile + 1, :]
-            else:
-                line = yr[FACE[1, ey].index(q) + (0 if ey == 1 else 7), xs : xs + 1, :]
-            plane = jnp.where(row == first_row, line, pltpu.roll(plane, ey % 16, 0))
-        if ez:
-            face = FACE[2, ez].index(q)
-            if outside:
-                edge = zx[0:16, :] if ex == 1 else zx[16:32, :]
-                block = 7 if ex == 1 else 0
-            else:
-                edge = zr[16 * (xs % 2) : 16 * (xs % 2) + 16, :]
-                block = xs // 2
-            at = 16 * block + 2 * face + (0 if ez == 1 else 1)
-            if ey:
-                beyond = zy[0 if ey == 1 else 1, 16 * (xs % 2) : 16 * (xs % 2) + 16, :]
-                edge = pltpu.roll(jnp.where(row == last_row, beyond, edge), ey % 16, 0)
-            goal = 0 if ez == 1 else 127
-            moved = pltpu.roll(edge, (goal - at) % 128, 1) if (goal - at) % 128 else edge
-            plane = jnp.where(lane == goal, moved, pltpu.roll(plane, ez % 128, 1))
-        store(x, plane)
-
-
-def running_kernel(
-    post_hbm, phi_hbm, x_hbm, y_hbm, z_hbm, zx_hbm, zy_hbm, c_hbm,
-    flow_out, pos_out, neg_out, phi_out,
-    post, moved, xr, yr, zr, zx, zy, cr, in_sem, out_sem, face_sem,
-):
-    def output(q):
-        if q < 19:
-            return flow_out.at[q]
-        return pos_out.at[q - 19] if q < 26 else neg_out.at[q - 26]
-
-    pairs = ((x_hbm, xr), (y_hbm, yr), (z_hbm, zr), (zx_hbm, zx), (zy_hbm, zy), (c_hbm, cr))
-    faces = [pltpu.make_async_copy(a, b, face_sem.at[n]) for n, (a, b) in enumerate(pairs)]
-    reads = [pltpu.make_async_copy(post_hbm.at[q], post.at[q], in_sem.at[q]) for q in range(33)]
-    writes = []
+def store_kernel(moved, phi, flow_out, pos_out, neg_out, phi_out, sem):
+    copies = [pltpu.make_async_copy(phi, phi_out, sem.at[33])]
     for q in range(33):
-        source = post if DIRS[q] == (0, 0, 0) else moved
-        writes.append(pltpu.make_async_copy(source.at[q], output(q), out_sem.at[q]))
-    writes.append(pltpu.make_async_copy(phi_hbm, phi_out, out_sem.at[33]))
-    for copy in (reads[0], *faces, *reads[1:], writes[33]):
+        target = flow_out.at[q] if q < 19 else pos_out.at[q - 19] if q < 26 else neg_out.at[q - 26]
+        copies.append(pltpu.make_async_copy(moved.at[q], target, sem.at[q]))
+    for copy in copies:
         copy.start()
-    for q in range(33):
-        reads[q].wait()
-        if q == 1:
-            for copy in faces:
-                copy.wait()
-        if DIRS[q] != (0, 0, 0):
-
-            def load(x, q=q):
-                return post[q, 16 * x : 16 * x + 16, :]
-
-            def store(x, plane, q=q):
-                moved[q, 16 * x : 16 * x + 16, :] = plane
-
-            run_population(q, load, xr, yr, zr, zx, zy, cr, store)
-        writes[q].start()
-    for copy in writes:
+    for copy in copies:
         copy.wait()
 
 
-def run_all(post, phi, faces):
-    anywhere = pl.BlockSpec(memory_space=pl.ANY)
+def store_all(moved, phi):
     shapes = [(19, 256, 128), (7, 256, 128), (7, 256, 128), (256, 128)]
     return pl.pallas_call(
-        running_kernel,
+        store_kernel,
         out_shape=[jax.ShapeDtypeStruct(s, f32) for s in shapes],
-        in_specs=[anywhere] * 8,
-        out_specs=[anywhere] * 4,
-        scratch_shapes=[pltpu.VMEM((33, 256, 128), f32)] * 2
-        + [pltpu.VMEM(s, f32) for s in FACE_SHAPES]
-        + [pltpu.SemaphoreType.DMA((n,)) for n in (33, 34, 6)],
-        compiler_params=pltpu.CompilerParams(vmem_limit_bytes=VMEM_LIMIT),
-        name="running",
-    )(post, phi, *faces)
+        in_specs=[pl.BlockSpec(memory_space=pltpu.VMEM)] * 2,
+        out_specs=[pl.BlockSpec(memory_space=pl.ANY)] * 4,
+        scratch_shapes=[pltpu.SemaphoreType.DMA((34,))],
+        compiler_params=pltpu.CompilerParams(vmem_limit_bytes=2 << 20),
+        name="results",
+    )(moved, phi)
 
 
 def shards(flow_pops, ion_pos, ion_neg, gray_class, fraction_table):
@@ -754,8 +730,8 @@
     ion_pos = ion_pos.reshape(7, 256, 128)
     ion_neg = ion_neg.reshape(7, 256, 128)
     gray = gray_class.reshape(256, 128)
-    post, phi, *faces = collide_all(fraction_table, flow_pops, ion_pos, ion_neg, gray)
-    flow_new, pos_new, neg_new, phi = run_all(post, phi, faces)
+    moved, phi = collide_all(fraction_table, flow_pops, ion_pos, ion_neg, gray)
+    flow_new, pos_new, neg_new, phi = store_all(moved, phi)
     return (
         flow_new.reshape(19, *extent),
         pos_new.reshape(7, *extent),

time: 55.2 us -> 51.6 us (0.935)
  Pallas kernels: 54.5 us -> 50.8 us
    pallas_call x2, Pallas kernels: 54.5 us -> 50.8 us  [the longest x1 48.5 us: collide_all(): pl.pallas_call(main_kernel, out_shape=[pltpu.VMEM(s, f32) for s in shapes...]
where the time goes in v3:
time: 51.6 us; the launch traced here: 51.5 us
  Pallas kernels  50.8 us (98%)
  between operations  0.64 us (1%)
    pallas_call x1, Pallas kernels, collide_all(): pl.pallas_call(main_kernel, out_shape=[pltpu.VMEM(s, f32) for s in shapes...  48.5 us
    pallas_call x1, Pallas kernels, store_all(): pl.pallas_call(store_kernel, out_shape=[jax.ShapeDtypeStruct(s, f32) for...  2.36 us

profile of v3, /device:TPU:1, one launch (start us, length us, event | category | flops | bytes accessed | tf_op | source)
XLA Modules:
  0.0 51.5 jit_solution(234499931989783977)
XLA Ops:
  0.6 48.5 %collision.1 = (f32[33,256,128]{2,1,0:T(8,128)S(1)}, f32[256,128]{1,0:T(8,128)S(1)}) custom-call(f32[16]{0:T(128)} %table_ref.1, f32[7,256,128]{2,1,0:T(8,128)} %bitcast.9, f32[7,256,128]{2,1,0:T(8,128)} %bitcast.10, f32[19,256,128]{2,1,0:T(8,128)} %bitcast.8, s32[256,128]{1,0:T(8,128)} %bitcast.11, f32[128,256]{1,0:T(8,128)} %constant.8.clone.hy_hbm, ...), custom_call_target="tpu_custom_call" | custom-call | tf_op jit(solution)/shard_map/collision/pallas_call | solution.py:687
  49.1 2.4 %results.1 = (f32[19,256,128]{2,1,0:T(8,128)}, f32[7,256,128]{2,1,0:T(8,128)}, f32[7,256,128]{2,1,0:T(8,128)}, f32[256,128]{1,0:T(8,128)}) custom-call(f32[33,256,128]{2,1,0:T(8,128)S(1)} %get-tuple-element.10.moved, f32[256,128]{1,0:T(8,128)S(1)} %get-tuple-element.11.phi), custom_call_target="tpu_custom_call" | custom-call | tf_op jit(solution)/shard_map/results/pallas_call | solution.py:716

commit v4 on v3

--- a/solution.py
+++ b/solution.py
@@ -60,6 +60,11 @@
     return cas_table64(points_k, points_n, length).astype(np.float32)
 
 
+def pack_rank(table, b):
+    part = table[:, 16 * b : 16 * b + 16].reshape(2, 8, 8, 16)
+    return part.transpose(0, 2, 1, 3).reshape(16, 128)
+
+
 def tables():
     hy = cas_table(np.arange(NY), np.arange(NY), NY)
     z = np.arange(NZ)
@@ -83,10 +88,11 @@
     for b in range(16):
         m = np.tile(mu[:, 16 * b : 16 * b + 16], (1, 8))
         c = np.tile(scale[:, 16 * b : 16 * b + 16], (1, 8))
-        packed = mu[:, 16 * b : 16 * b + 16].reshape(2, 8, 8, 16).transpose(0, 2, 1, 3).reshape(16, 128)
+        packed = pack_rank(mu, b)
         per_rank.append(
             np.concatenate(
-                [m, m ** (window + 1), m ** (8 - window), m**8, c, packed**16, 1.0 / (1.0 - packed**256)]
+                [m, m ** (window + 1), m ** (8 - window), m**8, c]
+                + [packed**16, 1.0 / (1.0 - packed**256), packed, pack_rank(scale, b)]
             )
         )
     return (
@@ -260,11 +266,20 @@
         left = packed(lax.rem(flow + 16 - d, 16), 0) + ratio * left
         right = packed(lax.rem(flow + d, 16), 16) + ratio * right
     left, right = left * image, right * image
+    one, packed_scale = gtab[672:688, :], gtab[688:704, :]
+    behind = packed_scale * (left + one * (packed(flow, 16) + ratio * right))
+    ahead = packed_scale * (right + one * (packed(flow, 0) + ratio * left))
+    small = window_of((8, 128))
     for tile in range(16):
         rows = slice(8 * tile, 8 * tile + 8)
         half = 8 * (tile // 8)
         from_left = spread(left[half : half + 8, :], tile % 8)
         from_right = spread(right[half : half + 8, :], tile % 8)
+        part, j = slice(half, half + 8), tile % 8
+        at_first, at_second = (-16 * j) % 128, (16 - 16 * j) % 128
+        first = pltpu.roll(behind[part, :], at_first, 1) if at_first else behind[part, :]
+        second = pltpu.roll(ahead[part, :], at_second, 1) if at_second else ahead[part, :]
+        out[rows, 256:384] = jnp.where(small == 0, first, jnp.where(small == 1, second, 0.0))
         near, far, eighth, scale = (
             gtab[128 * n + 8 * tile : 128 * n + 8 * tile + 8, :] for n in range(1, 5)
         )
@@ -279,19 +294,20 @@
         return gathered[40 * block + 32 + n : 40 * block + 33 + n, :]
 
     mean = sum((moment(n, 0) for n in range(1, 16)), moment(0, 0)) * (1.0 / NX)
-    first = second = left_sum = left_first = jnp.zeros((1, 128), f32)
+    moment_first = second_moment = left_sum = left_first = jnp.zeros((1, 128), f32)
     for block in range(16):
         centre = 16.0 * block - 120.0
         own = moment(block, 0) - 16.0 * mean
         own_first = centre * own + moment(block, 1)
-        first = first + own_first
-        second = second + (centre * own_first + centre * moment(block, 1))
-        second = second + (moment(block, 2) - 340.0 * mean)
+        moment_first = moment_first + own_first
+        second_moment = second_moment + (centre * own_first + centre * moment(block, 1))
+        second_moment = second_moment + (moment(block, 2) - 340.0 * mean)
         before = jnp.where(block < flow, 1.0, 0.0)
         left_sum = left_sum + before * own
         left_first = left_first + before * own_first
     window = window_of((8, 128)).astype(f32)
     centre = 16.0 * flow.astype(f32) - 120.0
+    start_sum, start_first = left_sum, left_first
     for g in range(2):
         at = centre + (window - 7.5 + 8.0 * g)
         zero = (rho_first[g] - mean) * mask
@@ -299,10 +315,45 @@
         upto, upto_first = left_sum + to_here, left_first + to_here_first
         left_sum = left_sum + spread(to_here, 7)
         left_first = left_first + spread(to_here_first, 7)
-        distance = 2.0 * (at * upto - upto_first) + first
-        value = (second - 2.0 * at * first) * (0.5 / NX) - 0.5 * distance
+        distance = 2.0 * (at * upto - upto_first) + moment_first
+        value = (second_moment - 2.0 * at * moment_first) * (0.5 / NX) - 0.5 * distance
         lanes = slice(128 * g, 128 * g + 128)
         out[0:8, lanes] = out[0:8, lanes] + (coupling / (NY * NZ)) * (mask * value)
+    at = centre - 8.5 + 17.0 * window
+    upto = jnp.where(small == 0, start_sum, left_sum)
+    upto_first = jnp.where(small == 0, start_first, left_first)
+    distance = 2.0 * (at * upto - upto_first) + moment_first
+    value = (second_moment - 2.0 * at * moment_first) * (0.5 / NX) - 0.5 * distance
+    value = jnp.where(small < 2, mask * value, 0.0)
+    out[0:8, 256:384] = out[0:8, 256:384] + (coupling / (NY * NZ)) * value
+
+
+def send_halo(modes_y, s1):
+    window = window_of((8, 128))
+    for pair in range(4):
+        tile = jnp.zeros((8, 128), f32)
+        for k in range(4):
+            piece = modes_y[pl.ds(32 * pair + k, 8, stride=4), :]
+            piece = pltpu.roll(piece, 32 * k, 1) if k else piece
+            tile = jnp.where(window // 2 == k, piece, tile)
+        for n in range(2):
+            at = 40 * (2 * pair + n) + 32
+            s1[at : at + 4, :] = tile[4 * n : 4 * n + 4, :]
+    for block in range(CY):
+        for side, (other, line) in enumerate((((block - 1) % CY, 15), ((block + 1) % CY, 0))):
+            for g in range(2):
+                to, at = 40 * block + 36 + 2 * side + g, 40 * other + 16 * g + line
+                s1[to : to + 1, :] = s1[at : at + 1, :]
+
+
+def receive_halo(rows, xh, yh):
+    for side in range(2):
+        for r in range(4):
+            at = 16 * side + 4 * r
+            xh[at : at + 4, :] = rows[pl.ds(8 * side + r, 4, stride=16), :]
+        for g in range(2):
+            at = 16 * side + 8 * g
+            yh[at : at + 8, :] = rows[pl.ds(4 + 2 * side + g, 8, stride=8), :]
 
 
 def pick_solid(gray, table_ref):
@@ -398,15 +449,28 @@
     lax.fori_loop(0, 32, block, 0)
 
 
-def gather_faces(post, xf, yf, zf, corner):
+def gather_corners(post, corner):
+    corner[0] = post[7, 248:256, :]
+    corner[1] = post[8, 0:8, :]
+    corner[2] = post[9, 240:248, :]
+    corner[3] = post[10, 8:16, :]
+
+
+def gather_x_faces(post, xf):
     for n, q in enumerate(FACE[0, 1]):
         xf[n] = post[q, 240:256, :]
     for n, q in enumerate(FACE[0, -1]):
         xf[7 + n] = post[q, 0:16, :]
+
+
+def gather_y_faces(post, yf):
     for n, q in enumerate(FACE[1, 1]):
         yf[n] = post[q, pl.ds(15, 16, stride=16), :]
     for n, q in enumerate(FACE[1, -1]):
         yf[7 + n] = post[q, pl.ds(0, 16, stride=16), :]
+
+
+def gather_z_faces(post, zf):
     lane = lax.broadcasted_iota(jnp.int32, (16, 128), 1)
     packed = [jnp.zeros((16, 128), f32), jnp.zeros((16, 128), f32)]
     for n, (up, down) in enumerate(zip(FACE[2, 1], FACE[2, -1])):
@@ -419,10 +483,6 @@
             packed[x % 2] = jnp.where((lane == at) | (lane == at + 1), moved, packed[x % 2])
     zf[0:16, :] = packed[0]
     zf[16:32, :] = packed[1]
-    corner[0] = post[7, 248:256, :]
-    corner[1] = post[8, 0:8, :]
-    corner[2] = post[9, 240:248, :]
-    corner[3] = post[10, 8:16, :]
 
 
 def face_messages(xf, yf, zf, corner, xr, yr, zr, zx, zy, cr):
@@ -517,9 +577,9 @@
     table_ref, pos_hbm, neg_hbm, flow_hbm, gray_hbm, hy_hbm, hz_hbm, back_hbm, gtab_hbm,
     moved, phi,
     pops, post, gray, hy_ref, hz_ref, back_ref, gtab, aux, field, charge,
-    s0, r0, moments, gathered, partial, modes, s1, r1, joined, ys, xh, yh,
+    s0, r0, moments, gathered, partial, modes, beside, s1, r1, joined, halo, xh, yh,
     xf, yf, zf, corner, xr, yr, zr, zx, zy, cr,
-    load_sem, send_sem, recv_sem, hsend_sem, hrecv_sem, fsend_sem, frecv_sem,
+    load_sem, send_sem, recv_sem, fsend_sem, frecv_sem,
 ):
     flow, cy, cz = place()
     me = cz * CY + cy
@@ -538,7 +598,7 @@
             )
         )
     ]
-    for copy in loads:
+    for copy in loads[:3]:
         copy.start()
     barrier = pltpu.get_barrier_semaphore()
 
@@ -568,6 +628,8 @@
         pos = pos + pops[19 + q]
         neg = neg + pops[26 + q]
     charge[...] = pos - neg
+    for copy in loads[3:]:
+        copy.start()
 
     spectrum = fdot(charge[...], hz_ref[...])
     for g in range(2):
@@ -605,72 +667,72 @@
     gathered_potential(
         [r[0:8, :] for r in rho], gtab, gathered, partial, mask, flow, modes
     )
-    s1[...] = fdot(hy_ref[:, 0:128], modes[...])
+    spectrum = fdot(hy_ref[:, 0:128], modes[...])
+    for block in range(CY):
+        for g in range(2):
+            at = 40 * block + 16 * g
+            s1[at : at + 16, :] = spectrum[16 * block : 16 * block + 16, 128 * g : 128 * g + 128]
+    beside[...] = spectrum[:, 256:384]
+    send_halo(beside, s1)
     swap_across_plane(
-        lambda b: rows_at(s1, 16 * lax.rem(b, CY), 16),
-        lambda b: rows_at(r1, 16 * b, 16),
+        lambda b: s1.at[pl.ds(pl.multiple_of(40 * lax.rem(b, CY), 8), 40), :],
+        lambda b: r1.at[pl.ds(pl.multiple_of(40 * b, 8), 40), :],
         send_sem.at[2],
         recv_sem.at[2],
     )
     settle(r1, recv_sem.at[2])
     for g in range(2):
         for c in range(2):
-            blocks = [
-                r1[128 * c + 16 * i : 128 * c + 16 * i + 16, 128 * g : 128 * g + 128]
-                for i in range(8)
-            ]
+            blocks = []
+            for i in range(8):
+                at = 40 * (8 * c + i) + 16 * g
+                blocks.append(r1[at : at + 16, :])
             for i, block in enumerate(swap_windows(blocks)):
                 at = 128 * g + 16 * i
                 joined[at : at + 16, 128 * c : 128 * c + 128] = block
-    both = fdot(joined[...], back_ref[...])
+    for c in range(2):
+        blocks = []
+        for i in range(8):
+            at = 40 * (8 * c + i) + 32
+            blocks.append(r1[at : at + 8, :])
+        for i, block in enumerate(swap_windows(blocks)):
+            joined[256 + 8 * i : 264 + 8 * i, 128 * c : 128 * c + 128] = block
+    both = fdot(joined[0:256, :], back_ref[...])
     phi[...] = both[:, :128]
     field[2] = both[:, 128:]
-
-    ahead, behind = lax.rem(flow + 1, FLOW), lax.rem(flow + FLOW - 1, FLOW)
-    above, below = lax.rem(cy + 1, CY), lax.rem(cy + CY - 1, CY)
-    copies = []
-
-    def halo(n, source, target, device):
-        copies.append(
-            pltpu.make_async_remote_copy(
-                src_ref=source,
-                dst_ref=target,
-                send_sem=hsend_sem.at[n],
-                recv_sem=hrecv_sem.at[n],
-                device_id=device,
-                device_id_type=MESH,
-            )
-        )
-        copies[-1].start()
-
-    halo(0, phi.at[pl.ds(240, 16), :], xh.at[pl.ds(0, 16), :], {"flow": ahead})
-    halo(1, phi.at[pl.ds(0, 16), :], xh.at[pl.ds(16, 16), :], {"flow": behind})
-    ys[0:16, :] = phi[pl.ds(15, 16, stride=16), :]
-    ys[16:32, :] = phi[pl.ds(0, 16, stride=16), :]
-    halo(2, ys.at[pl.ds(0, 16), :], yh.at[pl.ds(0, 16), :], {"cy": above})
-    halo(3, ys.at[pl.ds(16, 16), :], yh.at[pl.ds(16, 16), :], {"cy": below})
-    for copy in copies:
-        copy.wait()
+    halo[...] = fdot(joined[256:320, :], back_ref[:, 0:128])
+    receive_halo(halo, xh, yh)
     fill_fields(phi, xh, yh, field)
     finish(pops, aux, field, post)
-    gather_faces(post, xf, yf, zf, corner)
     copies = []
-    for n, (source, target, i, j, k) in enumerate(messages):
-        copies.append(
-            pltpu.make_async_remote_copy(
-                src_ref=source,
-                dst_ref=target,
-                send_sem=fsend_sem.at[n],
-                recv_sem=frecv_sem.at[n],
-                device_id=partner(i, j, k),
-                device_id_type=MESH,
+
+    def send_faces(first, last):
+        for n in range(first, last):
+            source, target, i, j, k = messages[n]
+            copies.append(
+                pltpu.make_async_remote_copy(
+                    src_ref=source,
+                    dst_ref=target,
+                    send_sem=fsend_sem.at[n],
+                    recv_sem=frecv_sem.at[n],
+                    device_id=partner(i, j, k),
+                    device_id_type=MESH,
+                )
             )
-        )
-        copies[-1].start()
+            copies[-1].start()
+
+    gather_corners(post, corner)
+    send_faces(9, 13)
+    gather_x_faces(post, xf)
+    send_faces(0, 2)
+    gather_y_faces(post, yf)
+    send_faces(2, 4)
+    gather_z_faces(post, zf)
+    send_faces(4, 9)
     run_inside(post, moved)
     settle(s0.at[pl.ds(0, 240), :], send_sem.at[0])
     settle(gathered.at[pl.ds(0, 600), :], send_sem.at[1])
-    settle(s0.at[pl.ds(0, 240), :], send_sem.at[2])
+    settle(gathered.at[pl.ds(0, 600), :], send_sem.at[2])
     for copy in copies:
         copy.wait()
     run_edges(moved, xr, yr, zr, zx, zy, cr)
@@ -680,9 +742,10 @@
     rows, square = (256, 128), (256, 256)
     anywhere = pl.BlockSpec(memory_space=pl.ANY)
     shapes = [(33, 256, 128), rows]
-    buffers = [(128, 256), (128, 256), square, (672, 128), (7, 256, 128), (3, 256, 128), rows]
-    buffers += [square, square, (40, 128), (640, 128), (2, 128, 128), (128, 256), (128, 256), square, square]
-    buffers += [(32, 128), (32, 128), (32, 128)]
+    buffers = [(128, 256), (128, 256), square, (704, 128), (7, 256, 128), (3, 256, 128), rows]
+    buffers += [square, square, (40, 128), (640, 128), (2, 128, 128), (128, 384)]
+    buffers += [(128, 128), (320, 128), (640, 128), (320, 256), (64, 128)]
+    buffers += [(32, 128), (32, 128)]
     buffers += [(14, 16, 128), (14, 16, 128), (32, 128), (4, 8, 128)] + FACE_SHAPES
     return pl.pallas_call(
         main_kernel,
@@ -692,7 +755,7 @@
         scratch_shapes=[pltpu.VMEM((33, 256, 128), f32)] * 2
         + [pltpu.VMEM(rows, jnp.int32)]
         + [pltpu.VMEM(s, f32) for s in buffers]
-        + [pltpu.SemaphoreType.DMA((n,)) for n in (8, 3, 3, 4, 4, 13, 13)],
+        + [pltpu.SemaphoreType.DMA((n,)) for n in (8, 3, 3, 13, 13)],
         compiler_params=pltpu.CompilerParams(
             collective_id=0, has_side_effects=True, vmem_limit_bytes=VMEM_LIMIT
         ),

time: 51.6 us -> 48.9 us (0.948)
  Pallas kernels: 50.8 us -> 48.1 us
    pallas_call x1, Pallas kernels: 48.5 us -> 45.8 us  [collide_all(): pl.pallas_call(main_kernel, out_shape=[pltpu.VMEM(s, f32) for s in shapes...]
where the time goes in v4:
time: 48.9 us; the launch traced here: 48.8 us
  Pallas kernels  48.1 us (98%)
  between operations  0.64 us (1%)
    pallas_call x1, Pallas kernels, collide_all(): pl.pallas_call(main_kernel, out_shape=[pltpu.VMEM(s, f32) for s in shapes...  45.8 us
    pallas_call x1, Pallas kernels, store_all(): pl.pallas_call(store_kernel, out_shape=[jax.ShapeDtypeStruct(s, f32) for...  2.36 us

profile of v4, /device:TPU:1, one launch (start us, length us, event | category | flops | bytes accessed | tf_op | source)
XLA Modules:
  0.0 48.8 jit_solution(11704794524156026593)
XLA Ops:
  0.6 45.8 %collision.1 = (f32[33,256,128]{2,1,0:T(8,128)S(1)}, f32[256,128]{1,0:T(8,128)S(1)}) custom-call(f32[16]{0:T(128)} %table_ref.1, f32[7,256,128]{2,1,0:T(8,128)} %bitcast.9, f32[7,256,128]{2,1,0:T(8,128)} %bitcast.10, f32[19,256,128]{2,1,0:T(8,128)} %bitcast.8, s32[256,128]{1,0:T(8,128)} %bitcast.11, f32[128,256]{1,0:T(8,128)} %constant.8.clone.hy_hbm, ...), custom_call_target="tpu_custom_call" | custom-call | tf_op jit(solution)/shard_map/collision/pallas_call | solution.py:750
  46.4 2.4 %results.1 = (f32[19,256,128]{2,1,0:T(8,128)}, f32[7,256,128]{2,1,0:T(8,128)}, f32[7,256,128]{2,1,0:T(8,128)}, f32[256,128]{1,0:T(8,128)}) custom-call(f32[33,256,128]{2,1,0:T(8,128)S(1)} %get-tuple-element.10.moved, f32[256,128]{1,0:T(8,128)S(1)} %get-tuple-element.11.phi), custom_call_target="tpu_custom_call" | custom-call | tf_op jit(solution)/shard_map/results/pallas_call | solution.py:779

commit v5 on v4

--- a/solution.py
+++ b/solution.py
@@ -412,41 +412,103 @@
     lax.fori_loop(0, 32, block, 0)
 
 
-def finish(pops, aux, field, post):
-    def block(i, carry):
-        at = pl.ds(pl.multiple_of(8 * i, 8), 8)
-        velocity = [aux[d, at, :] for d in range(3)]
-        electric = [field[d, at, :] for d in range(3)]
-        push = aux[3, at, :]
-        drift = [velocity[d] + push * electric[d] for d in range(3)]
-        square = drift[0] * drift[0] + drift[1] * drift[1] + drift[2] * drift[2]
-        mass = aux[4, at, :]
-        base = 1.0 - 1.5 * square
-        post[0, at, :] = pops[0, at, :] + (mass * flow_weights[0]) * base
-        for q in range(1, 19, 2):
-            along = None
-            for d in range(3):
-                if flow_dirs[q][d] and along is None:
-                    along = drift[d] if flow_dirs[q][d] == 1 else -drift[d]
-                elif flow_dirs[q][d]:
-                    along = along + drift[d] if flow_dirs[q][d] == 1 else along - drift[d]
-            scaled = mass * flow_weights[q]
-            even = scaled * (base + 4.5 * along * along)
-            odd = (3.0 * scaled) * along
+def drift_of(velocity, push, electric):
+    drift = [velocity[d] + push * electric[d] for d in range(3)]
+    return drift, 1.0 - 1.5 * (drift[0] * drift[0] + drift[1] * drift[1] + drift[2] * drift[2])
+
+
+def along_of(direction, drift):
+    along = None
+    for d in range(3):
+        if direction[d] and along is None:
+            along = drift[d] if direction[d] == 1 else -drift[d]
+        elif direction[d]:
+            along = along + drift[d] if direction[d] == 1 else along - drift[d]
+    return along
+
+
+def fluid_terms(mass, weight, base, along):
+    scaled = mass * weight
+    return scaled * (base + 4.5 * along * along), (3.0 * scaled) * along
+
+
+def finish_rows(at, pops, aux, field, post):
+    velocity = [aux[d, at, :] for d in range(3)]
+    electric = [field[d, at, :] for d in range(3)]
+    drift, base = drift_of(velocity, aux[3, at, :], electric)
+    mass = aux[4, at, :]
+    post[0, at, :] = pops[0, at, :] + (mass * flow_weights[0]) * base
+    for q in range(1, 19, 2):
+        even, odd = fluid_terms(mass, flow_weights[q], base, along_of(flow_dirs[q], drift))
+        post[q, at, :] = pops[q, at, :] + (even + odd)
+        post[q + 1, at, :] = pops[q + 1, at, :] + (even - odd)
+    for start, n, sign in ((19, 5, mobility), (26, 6, -mobility)):
+        mass = aux[n, at, :]
+        post[start, at, :] = pops[start, at, :] + ion_weights[0] * mass
+        even = ion_weights[1] * mass
+        for d in range(3):
+            q = start + 1 + 2 * d
+            odd = (4.0 * even) * (velocity[d] + sign * electric[d])
             post[q, at, :] = pops[q, at, :] + (even + odd)
             post[q + 1, at, :] = pops[q + 1, at, :] + (even - odd)
-        for start, n, sign in ((19, 5, mobility), (26, 6, -mobility)):
-            mass = aux[n, at, :]
-            post[start, at, :] = pops[start, at, :] + ion_weights[0] * mass
-            even = ion_weights[1] * mass
-            for d in range(3):
-                q = start + 1 + 2 * d
-                odd = (4.0 * even) * (velocity[d] + sign * electric[d])
-                post[q, at, :] = pops[q, at, :] + (even + odd)
-                post[q + 1, at, :] = pops[q + 1, at, :] + (even - odd)
-        return carry
-
-    lax.fori_loop(0, 32, block, 0)
+
+
+def pack_columns(planes):
+    lane = lax.broadcasted_iota(jnp.int32, (16, 128), 1)
+    packed = [jnp.zeros((16, 128), f32), jnp.zeros((16, 128), f32)]
+    for x in range(16):
+        up, down = planes(x, 0), planes(x, 1)
+        both = up if down is up else jnp.where(lane == 127, up, down)
+        moved = pltpu.roll(both, (16 * (x // 2) + 1) % 128, 1)
+        packed[x % 2] = jnp.where(lane // 16 == x // 2, moved, packed[x % 2])
+    return jnp.concatenate(packed, axis=0)
+
+
+def plane_at(x):
+    return slice(16 * x, 16 * x + 16)
+
+
+def pack_prepared(pops, aux, edge):
+    for n in range(7):
+        cache = {}
+
+        def planes(x, side, n=n, cache=cache):
+            if x not in cache:
+                cache[x] = aux[n, plane_at(x), :]
+            return cache[x]
+
+        edge[n] = pack_columns(planes)
+    for n, pair in enumerate(zip(FACE[2, 1], FACE[2, -1])):
+        edge[7 + n] = pack_columns(lambda x, side, pair=pair: pops[pair[side], plane_at(x), :])
+
+
+def z_faces(edge, field, zf):
+    lane = lax.broadcasted_iota(jnp.int32, (32, 128), 1)
+    sign = jnp.where(lane % 2 == 0, 1.0, -1.0)
+    electric = []
+    for d in range(3):
+        cache = {}
+
+        def planes(x, side, d=d, cache=cache):
+            if x not in cache:
+                cache[x] = field[d, plane_at(x), :]
+            return cache[x]
+
+        electric.append(pack_columns(planes))
+    velocity = [edge[d] for d in range(3)]
+    drift, base = drift_of(velocity, edge[3], electric)
+    out = jnp.zeros((32, 128), f32)
+    for n, q in enumerate(FACE[2, 1]):
+        if q < 19:
+            even, odd = fluid_terms(edge[4], flow_weights[q], base, along_of(flow_dirs[q], drift))
+        else:
+            which = 0 if q < 26 else 1
+            even = ion_weights[1] * edge[5 + which]
+            odd = (4.0 * even) * (velocity[2] + (mobility, -mobility)[which] * electric[2])
+        value = edge[7 + n] + (even + sign * odd)
+        moved = pltpu.roll(value, 2 * n, 1) if n else value
+        out = jnp.where((lane % 16) // 2 == n, moved, out)
+    zf[...] = out
 
 
 def gather_corners(post, corner):
@@ -468,21 +530,6 @@
         yf[n] = post[q, pl.ds(15, 16, stride=16), :]
     for n, q in enumerate(FACE[1, -1]):
         yf[7 + n] = post[q, pl.ds(0, 16, stride=16), :]
-
-
-def gather_z_faces(post, zf):
-    lane = lax.broadcasted_iota(jnp.int32, (16, 128), 1)
-    packed = [jnp.zeros((16, 128), f32), jnp.zeros((16, 128), f32)]
-    for n, (up, down) in enumerate(zip(FACE[2, 1], FACE[2, -1])):
-        for x in range(16):
-            both = jnp.where(
-                lane == 127, post[up, 16 * x : 16 * x + 16, :], post[down, 16 * x : 16 * x + 16, :]
-            )
-            at = 16 * (x // 2) + 2 * n
-            moved = pltpu.roll(both, (at + 1) % 128, 1)
-            packed[x % 2] = jnp.where((lane == at) | (lane == at + 1), moved, packed[x % 2])
-    zf[0:16, :] = packed[0]
-    zf[16:32, :] = packed[1]
 
 
 def face_messages(xf, yf, zf, corner, xr, yr, zr, zx, zy, cr):
@@ -576,7 +623,7 @@
 def main_kernel(
     table_ref, pos_hbm, neg_hbm, flow_hbm, gray_hbm, hy_hbm, hz_hbm, back_hbm, gtab_hbm,
     moved, phi,
-    pops, post, gray, hy_ref, hz_ref, back_ref, gtab, aux, field, charge,
+    pops, post, gray, hy_ref, hz_ref, back_ref, gtab, aux, field, charge, edge,
     s0, r0, moments, gathered, partial, modes, beside, s1, r1, joined, halo, xh, yh,
     xf, yf, zf, corner, xr, yr, zr, zx, zy, cr,
     load_sem, send_sem, recv_sem, fsend_sem, frecv_sem,
@@ -602,23 +649,11 @@
         copy.start()
     barrier = pltpu.get_barrier_semaphore()
 
-    def greet(k, carry):
-        other = lax.rem(me + k, 16)
-        pl.semaphore_signal(
-            barrier,
-            inc=1,
-            device_id={"cy": lax.rem(other, CY), "cz": lax.div(other, CY)},
-            device_id_type=MESH,
-        )
-        pl.semaphore_signal(
-            barrier, inc=1, device_id={"flow": lax.rem(flow + k, 16)}, device_id_type=MESH
-        )
-        return carry
-
-    lax.fori_loop(1, 16, greet, 0)
     messages = face_messages(xf, yf, zf, corner, xr, yr, zr, zx, zy, cr)
     strangers = [m[2:] for m in messages if m[2] and (m[3] or m[4])]
-    for i, j, k in strangers:
+    friends = [(0, j, k) for j in (4, 5, 3, 2, 6, 7, 1, 0) for k in (1, 0) if j or k]
+    friends += [(i, 0, 0) for i in (10, 6, 5, 11, 9, 7, 2, 14, 8, 3, 13, 12, 4, 15, 1)]
+    for i, j, k in strangers + friends:
         pl.semaphore_signal(barrier, inc=1, device_id=partner(i, j, k), device_id_type=MESH)
     for copy in loads[:3]:
         copy.wait()
@@ -651,6 +686,7 @@
     for copy in loads[3:]:
         copy.wait()
     prepare(pops, charge, gray, table_ref, aux)
+    pack_prepared(pops, aux, edge)
     settle(r0, recv_sem.at[0])
     spectrum = fdot(hy_ref[...], r0[...])
     rho = [spectrum[:, :128], spectrum[:, 128:]]
@@ -703,7 +739,8 @@
     halo[...] = fdot(joined[256:320, :], back_ref[:, 0:128])
     receive_halo(halo, xh, yh)
     fill_fields(phi, xh, yh, field)
-    finish(pops, aux, field, post)
+    for start in (0, 8, 240, 248):
+        finish_rows(pl.ds(start, 8), pops, aux, field, post)
     copies = []
 
     def send_faces(first, last):
@@ -725,10 +762,18 @@
     send_faces(9, 13)
     gather_x_faces(post, xf)
     send_faces(0, 2)
+    for start in (0, 15, 128, 143):
+        finish_rows(pl.ds(start, 8, stride=16), pops, aux, field, post)
     gather_y_faces(post, yf)
     send_faces(2, 4)
-    gather_z_faces(post, zf)
+    z_faces(edge, field, zf)
     send_faces(4, 9)
+
+    def finish_block(i, carry):
+        finish_rows(pl.ds(pl.multiple_of(8 * i, 8), 8), pops, aux, field, post)
+        return carry
+
+    lax.fori_loop(2, 30, finish_block, 0)
     run_inside(post, moved)
     settle(s0.at[pl.ds(0, 240), :], send_sem.at[0])
     settle(gathered.at[pl.ds(0, 600), :], send_sem.at[1])
@@ -743,6 +788,7 @@
     anywhere = pl.BlockSpec(memory_space=pl.ANY)
     shapes = [(33, 256, 128), rows]
     buffers = [(128, 256), (128, 256), square, (704, 128), (7, 256, 128), (3, 256, 128), rows]
+    buffers += [(14, 32, 128)]
     buffers += [square, square, (40, 128), (640, 128), (2, 128, 128), (128, 384)]
     buffers += [(128, 128), (320, 128), (640, 128), (320, 256), (64, 128)]
     buffers += [(32, 128), (32, 128)]

time: 48.9 us -> 47.2 us (0.965)
  Pallas kernels: 48.1 us -> 46.4 us
    pallas_call x1, Pallas kernels: 45.8 us -> 44 us  [collide_all(): pl.pallas_call(main_kernel, out_shape=[pltpu.VMEM(s, f32) for s in shapes...]
where the time goes in v5:
time: 47.2 us; the launch traced here: 47.1 us
  Pallas kernels  46.4 us (98%)
  between operations  0.64 us (1%)
    pallas_call x1, Pallas kernels, collide_all(): pl.pallas_call(main_kernel, out_shape=[pltpu.VMEM(s, f32) for s in shapes...  44 us
    pallas_call x1, Pallas kernels, store_all(): pl.pallas_call(store_kernel, out_shape=[jax.ShapeDtypeStruct(s, f32) for...  2.36 us

profile of v5, /device:TPU:1, one launch (start us, length us, event | category | flops | bytes accessed | tf_op | source)
XLA Modules:
  0.0 47.1 jit_solution(11546243848822271807)
XLA Ops:
  0.6 44.0 %collision.1 = (f32[33,256,128]{2,1,0:T(8,128)S(1)}, f32[256,128]{1,0:T(8,128)S(1)}) custom-call(f32[16]{0:T(128)} %table_ref.1, f32[7,256,128]{2,1,0:T(8,128)} %bitcast.9, f32[7,256,128]{2,1,0:T(8,128)} %bitcast.10, f32[19,256,128]{2,1,0:T(8,128)} %bitcast.8, s32[256,128]{1,0:T(8,128)} %bitcast.11, f32[128,256]{1,0:T(8,128)} %constant.8.clone.hy_hbm, ...), custom_call_target="tpu_custom_call" | custom-call | tf_op jit(solution)/shard_map/collision/pallas_call | solution.py:796
  44.7 2.4 %results.1 = (f32[19,256,128]{2,1,0:T(8,128)}, f32[7,256,128]{2,1,0:T(8,128)}, f32[7,256,128]{2,1,0:T(8,128)}, f32[256,128]{1,0:T(8,128)}) custom-call(f32[33,256,128]{2,1,0:T(8,128)S(1)} %get-tuple-element.10.moved, f32[256,128]{1,0:T(8,128)S(1)} %get-tuple-element.11.phi), custom_call_target="tpu_custom_call" | custom-call | tf_op jit(solution)/shard_map/results/pallas_call | solution.py:825

commit v6 on v5

--- a/solution.py
+++ b/solution.py
@@ -233,10 +233,8 @@
     return jnp.where((row == 0) & (lane % 16 == 0), here, 0.0)
 
 
-def block_moments(rho, gtab, moments, partial, mask):
-    mu, near, far, eighth = (gtab[128 * n : 128 * n + 128, :] for n in range(4))
-    up = [scan_up(r, mu) for r in rho]
-    down = [scan_down(r, mu) for r in rho]
+def block_moments(rho, up, down, gtab, moments, partial, mask):
+    near, far, eighth = (gtab[128 * n : 128 * n + 128, :] for n in range(1, 4))
     moments[0:16, :] = pack_windows(up[1] + eighth * up[0], 7)
     moments[16:32, :] = pack_windows(down[0] + eighth * down[1], 0)
     window = window_of((8, 128)).astype(f32)
@@ -328,7 +326,7 @@
     out[0:8, 256:384] = out[0:8, 256:384] + (coupling / (NY * NZ)) * value
 
 
-def send_halo(modes_y, s1):
+def send_halo(modes_y, s1, s2):
     window = window_of((8, 128))
     for pair in range(4):
         tile = jnp.zeros((8, 128), f32)
@@ -337,13 +335,14 @@
             piece = pltpu.roll(piece, 32 * k, 1) if k else piece
             tile = jnp.where(window // 2 == k, piece, tile)
         for n in range(2):
-            at = 40 * (2 * pair + n) + 32
-            s1[at : at + 4, :] = tile[4 * n : 4 * n + 4, :]
+            at = 24 * (2 * pair + n) + 16
+            s2[at : at + 4, :] = tile[4 * n : 4 * n + 4, :]
     for block in range(CY):
         for side, (other, line) in enumerate((((block - 1) % CY, 15), ((block + 1) % CY, 0))):
             for g in range(2):
-                to, at = 40 * block + 36 + 2 * side + g, 40 * other + 16 * g + line
-                s1[to : to + 1, :] = s1[at : at + 1, :]
+                source, at = (s1, 16 * other + line) if g == 0 else (s2, 24 * other + line)
+                to = 24 * block + 20 + 2 * side + g
+                s2[to : to + 1, :] = source[at : at + 1, :]
 
 
 def receive_halo(rows, xh, yh):
@@ -574,32 +573,41 @@
                 moved[q, 16 * x : 16 * x + 16, :] = plane
 
 
-def run_edges(moved, xr, yr, zr, zx, zy, cr):
-    lane = lax.broadcasted_iota(jnp.int32, (16, 128), 1)
-    row = lax.broadcasted_iota(jnp.int32, (16, 128), 0)
-    for q in range(1, 33):
-        ex, ey, ez = DIRS[q]
+def run_x_edges(moved, xr):
+    for ex in (1, -1):
         edge_x = 0 if ex == 1 else 15
-        first_row, last_row = (0, 15) if ey == 1 else (15, 0)
-        if ex:
-            plane = xr[FACE[0, ex].index(q) + (0 if ex == 1 else 7)]
+        for n, q in enumerate(FACE[0, ex]):
+            _, ey, ez = DIRS[q]
+            plane = xr[n + (0 if ex == 1 else 7)]
             if ey:
                 plane = pltpu.roll(plane, ey % 16, 0)
             if ez:
                 plane = pltpu.roll(plane, ez % 128, 1)
             moved[q, 16 * edge_x : 16 * edge_x + 16, :] = plane
-        if ey:
-            lines = yr[FACE[1, ey].index(q) + (0 if ey == 1 else 7)]
+
+
+def run_y_edges(moved, yr, cr):
+    row = lax.broadcasted_iota(jnp.int32, (16, 128), 0)
+    for ey in (1, -1):
+        for n, q in enumerate(FACE[1, ey]):
+            ex, _, ez = DIRS[q]
+            lines = yr[n + (0 if ey == 1 else 7)]
             if ex:
-                n = {7: 0, 8: 1, 9: 2, 10: 3}[q]
                 tile = 7 if ey == 1 else 0
-                lines = jnp.where(row == edge_x, cr[n, tile : tile + 1, :], pltpu.roll(lines, ex % 16, 0))
+                line = cr[q - 7, tile : tile + 1, :]
+                lines = jnp.where(row == (0 if ex == 1 else 15), line, pltpu.roll(lines, ex % 16, 0))
             if ez:
                 lines = pltpu.roll(lines, ez % 128, 1)
-            moved[q, pl.ds(first_row, 16, stride=16), :] = lines
-        if ez:
-            face = FACE[2, ez].index(q)
-            goal = 0 if ez == 1 else 127
+            moved[q, pl.ds(0 if ey == 1 else 15, 16, stride=16), :] = lines
+
+
+def run_z_edges(moved, zr, zx, zy):
+    lane = lax.broadcasted_iota(jnp.int32, (16, 128), 1)
+    row = lax.broadcasted_iota(jnp.int32, (16, 128), 0)
+    for ez in (1, -1):
+        goal = 0 if ez == 1 else 127
+        for face, q in enumerate(FACE[2, ez]):
+            ex, ey, _ = DIRS[q]
             for x in range(16):
                 xs = x - ex
                 if 0 <= xs <= 15:
@@ -610,6 +618,7 @@
                     block = 7 if ex == 1 else 0
                 if ey:
                     beyond = zy[0 if ey == 1 else 1, 16 * (xs % 2) : 16 * (xs % 2) + 16, :]
+                    last_row = 15 if ey == 1 else 0
                     edge = pltpu.roll(jnp.where(row == last_row, beyond, edge), ey % 16, 0)
                 shift = (goal - (16 * block + 2 * face + (0 if ez == 1 else 1))) % 128
                 column = pltpu.roll(edge, shift, 1) if shift else edge
@@ -624,7 +633,7 @@
     table_ref, pos_hbm, neg_hbm, flow_hbm, gray_hbm, hy_hbm, hz_hbm, back_hbm, gtab_hbm,
     moved, phi,
     pops, post, gray, hy_ref, hz_ref, back_ref, gtab, aux, field, charge, edge,
-    s0, r0, moments, gathered, partial, modes, beside, s1, r1, joined, halo, xh, yh,
+    s0, r0, moments, gathered, partial, modes, beside, s1, r1, s2, r2, joined, halo, xh, yh,
     xf, yf, zf, corner, xr, yr, zr, zx, zy, cr,
     load_sem, send_sem, recv_sem, fsend_sem, frecv_sem,
 ):
@@ -675,88 +684,95 @@
             ]
             for i, block in enumerate(swap_windows(blocks)):
                 at = 16 * (8 * c + i)
-                s0[at : at + 16, 128 * g : 128 * g + 128] = block
+                s0[g, at : at + 16, :] = block
     pl.semaphore_wait(barrier, 30 + len(strangers))
-    swap_across_plane(
-        lambda b: rows_at(s0, 16 * b, 16),
-        lambda b: rows_at(r0, 16 * b, 16),
-        send_sem.at[0],
-        recv_sem.at[0],
-    )
+    for g in range(2):
+        swap_across_plane(
+            lambda b, g=g: rows_at(s0.at[g], 16 * b, 16),
+            lambda b, g=g: rows_at(r0.at[g], 16 * b, 16),
+            send_sem.at[g],
+            recv_sem.at[g],
+        )
     for copy in loads[3:]:
         copy.wait()
     prepare(pops, charge, gray, table_ref, aux)
     pack_prepared(pops, aux, edge)
-    settle(r0, recv_sem.at[0])
-    spectrum = fdot(hy_ref[...], r0[...])
-    rho = [spectrum[:, :128], spectrum[:, 128:]]
+    rho, up, down = [], [], []
+    for g in range(2):
+        settle(r0.at[g], recv_sem.at[g])
+        rho.append(fdot(hy_ref[...], r0[g]))
+        up.append(scan_up(rho[g], gtab[0:128, :]))
+        down.append(scan_down(rho[g], gtab[0:128, :]))
     mask = zero_mode_mask(cy, cz)
-    rest = block_moments(rho, gtab, moments, partial, mask)
+    rest = block_moments(rho, up, down, gtab, moments, partial, mask)
     swap_along_flow(
         lambda a: moments,
         lambda a: gathered.at[pl.ds(pl.multiple_of(40 * a, 8), 40), :],
-        send_sem.at[1],
-        recv_sem.at[1],
+        send_sem.at[2],
+        recv_sem.at[2],
     )
     rest()
-    settle(gathered, recv_sem.at[1])
+    settle(gathered, recv_sem.at[2])
     gathered_potential(
         [r[0:8, :] for r in rho], gtab, gathered, partial, mask, flow, modes
     )
-    spectrum = fdot(hy_ref[:, 0:128], modes[...])
+    s1[...] = fdot(hy_ref[:, 0:128], modes[:, 0:128])
+    swap_across_plane(
+        lambda b: rows_at(s1, 16 * lax.rem(b, CY), 16),
+        lambda b: rows_at(r1, 16 * b, 16),
+        send_sem.at[3],
+        recv_sem.at[3],
+    )
+    spectrum = fdot(hy_ref[:, 0:128], modes[:, 128:384])
     for block in range(CY):
-        for g in range(2):
-            at = 40 * block + 16 * g
-            s1[at : at + 16, :] = spectrum[16 * block : 16 * block + 16, 128 * g : 128 * g + 128]
-    beside[...] = spectrum[:, 256:384]
-    send_halo(beside, s1)
+        s2[24 * block : 24 * block + 16, :] = spectrum[16 * block : 16 * block + 16, 0:128]
+    beside[...] = spectrum[:, 128:256]
+    send_halo(beside, s1, s2)
     swap_across_plane(
-        lambda b: s1.at[pl.ds(pl.multiple_of(40 * lax.rem(b, CY), 8), 40), :],
-        lambda b: r1.at[pl.ds(pl.multiple_of(40 * b, 8), 40), :],
-        send_sem.at[2],
-        recv_sem.at[2],
+        lambda b: s2.at[pl.ds(pl.multiple_of(24 * lax.rem(b, CY), 8), 24), :],
+        lambda b: r2.at[pl.ds(pl.multiple_of(24 * b, 8), 24), :],
+        send_sem.at[4],
+        recv_sem.at[4],
     )
-    settle(r1, recv_sem.at[2])
-    for g in range(2):
+    for g, (ref, step) in enumerate(((r1, 16), (r2, 24))):
+        settle(ref, recv_sem.at[3 + g])
         for c in range(2):
             blocks = []
             for i in range(8):
-                at = 40 * (8 * c + i) + 16 * g
-                blocks.append(r1[at : at + 16, :])
+                at = step * (8 * c + i)
+                blocks.append(ref[at : at + 16, :])
             for i, block in enumerate(swap_windows(blocks)):
                 at = 128 * g + 16 * i
                 joined[at : at + 16, 128 * c : 128 * c + 128] = block
+        both = fdot(joined[128 * g : 128 * g + 128, :], back_ref[...])
+        phi[128 * g : 128 * g + 128, :] = both[:, :128]
+        field[2, 128 * g : 128 * g + 128, :] = both[:, 128:]
     for c in range(2):
         blocks = []
         for i in range(8):
-            at = 40 * (8 * c + i) + 32
-            blocks.append(r1[at : at + 8, :])
+            at = 24 * (8 * c + i) + 16
+            blocks.append(r2[at : at + 8, :])
         for i, block in enumerate(swap_windows(blocks)):
             joined[256 + 8 * i : 264 + 8 * i, 128 * c : 128 * c + 128] = block
-    both = fdot(joined[0:256, :], back_ref[...])
-    phi[...] = both[:, :128]
-    field[2] = both[:, 128:]
     halo[...] = fdot(joined[256:320, :], back_ref[:, 0:128])
     receive_halo(halo, xh, yh)
     fill_fields(phi, xh, yh, field)
     for start in (0, 8, 240, 248):
         finish_rows(pl.ds(start, 8), pops, aux, field, post)
-    copies = []
+    copies = {}
 
     def send_faces(first, last):
         for n in range(first, last):
             source, target, i, j, k = messages[n]
-            copies.append(
-                pltpu.make_async_remote_copy(
-                    src_ref=source,
-                    dst_ref=target,
-                    send_sem=fsend_sem.at[n],
-                    recv_sem=frecv_sem.at[n],
-                    device_id=partner(i, j, k),
-                    device_id_type=MESH,
-                )
+            copies[n] = pltpu.make_async_remote_copy(
+                src_ref=source,
+                dst_ref=target,
+                send_sem=fsend_sem.at[n],
+                recv_sem=frecv_sem.at[n],
+                device_id=partner(i, j, k),
+                device_id_type=MESH,
             )
-            copies[-1].start()
+            copies[n].start()
 
     gather_corners(post, corner)
     send_faces(9, 13)
@@ -775,12 +791,20 @@
 
     lax.fori_loop(2, 30, finish_block, 0)
     run_inside(post, moved)
-    settle(s0.at[pl.ds(0, 240), :], send_sem.at[0])
-    settle(gathered.at[pl.ds(0, 600), :], send_sem.at[1])
+    for n in range(2):
+        settle(s0.at[n, pl.ds(0, 240), :], send_sem.at[n])
     settle(gathered.at[pl.ds(0, 600), :], send_sem.at[2])
-    for copy in copies:
-        copy.wait()
-    run_edges(moved, xr, yr, zr, zx, zy, cr)
+    settle(gathered.at[pl.ds(0, 240), :], send_sem.at[3])
+    settle(gathered.at[pl.ds(0, 360), :], send_sem.at[4])
+    for n in (0, 1):
+        copies[n].wait()
+    run_x_edges(moved, xr)
+    for n in (2, 3, 9, 10, 11, 12):
+        copies[n].wait()
+    run_y_edges(moved, yr, cr)
+    for n in (4, 5, 6, 7, 8):
+        copies[n].wait()
+    run_z_edges(moved, zr, zx, zy)
 
 
 def collide_all(table, flow_pops, ion_pos, ion_neg, gray):
@@ -789,8 +813,8 @@
     shapes = [(33, 256, 128), rows]
     buffers = [(128, 256), (128, 256), square, (704, 128), (7, 256, 128), (3, 256, 128), rows]
     buffers += [(14, 32, 128)]
-    buffers += [square, square, (40, 128), (640, 128), (2, 128, 128), (128, 384)]
-    buffers += [(128, 128), (320, 128), (640, 128), (320, 256), (64, 128)]
+    buffers += [(2, 256, 128), (2, 256, 128), (40, 128), (640, 128), (2, 128, 128), (128, 384)]
+    buffers += [(128, 128), (128, 128), rows, (192, 128), (384, 128), (320, 256), (64, 128)]
     buffers += [(32, 128), (32, 128)]
     buffers += [(14, 16, 128), (14, 16, 128), (32, 128), (4, 8, 128)] + FACE_SHAPES
     return pl.pallas_call(
@@ -801,7 +825,7 @@
         scratch_shapes=[pltpu.VMEM((33, 256, 128), f32)] * 2
         + [pltpu.VMEM(rows, jnp.int32)]
         + [pltpu.VMEM(s, f32) for s in buffers]
-        + [pltpu.SemaphoreType.DMA((n,)) for n in (8, 3, 3, 13, 13)],
+        + [pltpu.SemaphoreType.DMA((n,)) for n in (8, 5, 5, 13, 13)],
         compiler_params=pltpu.CompilerParams(
             collective_id=0, has_side_effects=True, vmem_limit_bytes=VMEM_LIMIT
         ),
@@ -809,11 +833,13 @@
     )(table, ion_pos, ion_neg, flow_pops, gray, *(jnp.asarray(t) for t in tables()))
 
 
+STORES = ((0, 4), (4, 4), (8, 4), (12, 4), (16, 3))
+
+
 def store_kernel(moved, phi, flow_out, pos_out, neg_out, phi_out, sem):
-    copies = [pltpu.make_async_copy(phi, phi_out, sem.at[33])]
-    for q in range(33):
-        target = flow_out.at[q] if q < 19 else pos_out.at[q - 19] if q < 26 else neg_out.at[q - 26]
-        copies.append(pltpu.make_async_copy(moved.at[q], target, sem.at[q]))
+    parts = [(moved.at[pl.ds(q, n)], flow_out.at[pl.ds(q, n)]) for q, n in STORES]
+    parts += [(moved.at[pl.ds(19, 7)], pos_out), (moved.at[pl.ds(26, 7)], neg_out), (phi, phi_out)]
+    copies = [pltpu.make_async_copy(a, b, sem.at[n]) for n, (a, b) in enumerate(parts)]
     for copy in copies:
         copy.start()
     for copy in copies:
@@ -827,7 +853,7 @@
         out_shape=[jax.ShapeDtypeStruct(s, f32) for s in shapes],
         in_specs=[pl.BlockSpec(memory_space=pltpu.VMEM)] * 2,
         out_specs=[pl.BlockSpec(memory_space=pl.ANY)] * 4,
-        scratch_shapes=[pltpu.SemaphoreType.DMA((34,))],
+        scratch_shapes=[pltpu.SemaphoreType.DMA((8,))],
         compiler_params=pltpu.CompilerParams(vmem_limit_bytes=2 << 20),
         name="results",
     )(moved, phi)

time: 47.2 us -> 46.9 us (level)
  no operation moved by 1% of the time
where the time goes in v6:
time: 46.9 us; the launch traced here: 46.8 us
  Pallas kernels  46.1 us (98%)
  between operations  0.64 us (1%)
    pallas_call x1, Pallas kernels, collide_all(): pl.pallas_call(main_kernel, out_shape=[pltpu.VMEM(s, f32) for s in shapes...  44 us
    pallas_call x1, Pallas kernels, store_all(): pl.pallas_call(store_kernel, out_shape=[jax.ShapeDtypeStruct(s, f32) for...  2.15 us

profile of v6, /device:TPU:1, one launch (start us, length us, event | category | flops | bytes accessed | tf_op | source)
XLA Modules:
  0.0 46.8 jit_solution(17255598570734301694)
XLA Ops:
  0.6 44.0 %collision.1 = (f32[33,256,128]{2,1,0:T(8,128)S(1)}, f32[256,128]{1,0:T(8,128)S(1)}) custom-call(f32[16]{0:T(128)} %table_ref.1, f32[7,256,128]{2,1,0:T(8,128)} %bitcast.9, f32[7,256,128]{2,1,0:T(8,128)} %bitcast.10, f32[19,256,128]{2,1,0:T(8,128)} %bitcast.8, s32[256,128]{1,0:T(8,128)} %bitcast.11, f32[128,256]{1,0:T(8,128)} %constant.8.clone.hy_hbm, ...), custom_call_target="tpu_custom_call" | custom-call | tf_op jit(solution)/shard_map/collision/pallas_call | solution.py:820
  44.6 2.2 %results.1 = (f32[19,256,128]{2,1,0:T(8,128)}, f32[7,256,128]{2,1,0:T(8,128)}, f32[7,256,128]{2,1,0:T(8,128)}, f32[256,128]{1,0:T(8,128)}) custom-call(f32[33,256,128]{2,1,0:T(8,128)S(1)} %get-tuple-element.10.moved, f32[256,128]{1,0:T(8,128)S(1)} %get-tuple-element.11.phi), custom_call_target="tpu_custom_call" | custom-call | tf_op jit(solution)/shard_map/results/pallas_call | solution.py:851

commit v7 on v6

--- a/solution.py
+++ b/solution.py
@@ -141,11 +141,13 @@
     pltpu.make_async_copy(source(me), target(me), recv_sem).start()
 
 
+FLOW_STEPS = (10, 6, 5, 11, 9, 7, 2, 14, 8, 3, 13, 12, 4, 15, 1)
+
+
 def swap_along_flow(source, target, send_sem, recv_sem):
     me, _, _ = place()
-
-    def step(k, carry):
-        other = lax.rem(me + k, 16)
+    for step in FLOW_STEPS:
+        other = lax.rem(me + step, FLOW)
         pltpu.make_async_remote_copy(
             src_ref=source(other),
             dst_ref=target(me),
@@ -154,9 +156,6 @@
             device_id={"flow": other},
             device_id_type=MESH,
         ).start()
-        return carry
-
-    lax.fori_loop(1, 16, step, 0)
     pltpu.make_async_copy(source(me), target(me), recv_sem).start()
 
 
@@ -661,7 +660,7 @@
     messages = face_messages(xf, yf, zf, corner, xr, yr, zr, zx, zy, cr)
     strangers = [m[2:] for m in messages if m[2] and (m[3] or m[4])]
     friends = [(0, j, k) for j in (4, 5, 3, 2, 6, 7, 1, 0) for k in (1, 0) if j or k]
-    friends += [(i, 0, 0) for i in (10, 6, 5, 11, 9, 7, 2, 14, 8, 3, 13, 12, 4, 15, 1)]
+    friends += [(i, 0, 0) for i in FLOW_STEPS]
     for i, j, k in strangers + friends:
         pl.semaphore_signal(barrier, inc=1, device_id=partner(i, j, k), device_id_type=MESH)
     for copy in loads[:3]:
@@ -686,20 +685,19 @@
                 at = 16 * (8 * c + i)
                 s0[g, at : at + 16, :] = block
     pl.semaphore_wait(barrier, 30 + len(strangers))
-    for g in range(2):
-        swap_across_plane(
-            lambda b, g=g: rows_at(s0.at[g], 16 * b, 16),
-            lambda b, g=g: rows_at(r0.at[g], 16 * b, 16),
-            send_sem.at[g],
-            recv_sem.at[g],
-        )
+    swap_across_plane(
+        lambda b: s0.at[:, pl.ds(pl.multiple_of(16 * b, 16), 16), :],
+        lambda b: r0.at[:, pl.ds(pl.multiple_of(16 * b, 16), 16), :],
+        send_sem.at[0],
+        recv_sem.at[0],
+    )
     for copy in loads[3:]:
         copy.wait()
     prepare(pops, charge, gray, table_ref, aux)
     pack_prepared(pops, aux, edge)
     rho, up, down = [], [], []
+    settle(r0, recv_sem.at[0])
     for g in range(2):
-        settle(r0.at[g], recv_sem.at[g])
         rho.append(fdot(hy_ref[...], r0[g]))
         up.append(scan_up(rho[g], gtab[0:128, :]))
         down.append(scan_down(rho[g], gtab[0:128, :]))
@@ -708,11 +706,11 @@
     swap_along_flow(
         lambda a: moments,
         lambda a: gathered.at[pl.ds(pl.multiple_of(40 * a, 8), 40), :],
-        send_sem.at[2],
-        recv_sem.at[2],
+        send_sem.at[1],
+        recv_sem.at[1],
     )
     rest()
-    settle(gathered, recv_sem.at[2])
+    settle(gathered, recv_sem.at[1])
     gathered_potential(
         [r[0:8, :] for r in rho], gtab, gathered, partial, mask, flow, modes
     )
@@ -720,8 +718,8 @@
     swap_across_plane(
         lambda b: rows_at(s1, 16 * lax.rem(b, CY), 16),
         lambda b: rows_at(r1, 16 * b, 16),
-        send_sem.at[3],
-        recv_sem.at[3],
+        send_sem.at[2],
+        recv_sem.at[2],
     )
     spectrum = fdot(hy_ref[:, 0:128], modes[:, 128:384])
     for block in range(CY):
@@ -731,11 +729,11 @@
     swap_across_plane(
         lambda b: s2.at[pl.ds(pl.multiple_of(24 * lax.rem(b, CY), 8), 24), :],
         lambda b: r2.at[pl.ds(pl.multiple_of(24 * b, 8), 24), :],
-        send_sem.at[4],
-        recv_sem.at[4],
+        send_sem.at[3],
+        recv_sem.at[3],
     )
     for g, (ref, step) in enumerate(((r1, 16), (r2, 24))):
-        settle(ref, recv_sem.at[3 + g])
+        settle(ref, recv_sem.at[2 + g])
         for c in range(2):
             blocks = []
             for i in range(8):
@@ -791,11 +789,10 @@
 
     lax.fori_loop(2, 30, finish_block, 0)
     run_inside(post, moved)
-    for n in range(2):
-        settle(s0.at[n, pl.ds(0, 240), :], send_sem.at[n])
-    settle(gathered.at[pl.ds(0, 600), :], send_sem.at[2])
-    settle(gathered.at[pl.ds(0, 240), :], send_sem.at[3])
-    settle(gathered.at[pl.ds(0, 360), :], send_sem.at[4])
+    settle(s0.at[:, pl.ds(0, 240), :], send_sem.at[0])
+    settle(gathered.at[pl.ds(0, 600), :], send_sem.at[1])
+    settle(gathered.at[pl.ds(0, 240), :], send_sem.at[2])
+    settle(gathered.at[pl.ds(0, 360), :], send_sem.at[3])
     for n in (0, 1):
         copies[n].wait()
     run_x_edges(moved, xr)
@@ -825,7 +822,7 @@
         scratch_shapes=[pltpu.VMEM((33, 256, 128), f32)] * 2
         + [pltpu.VMEM(rows, jnp.int32)]
         + [pltpu.VMEM(s, f32) for s in buffers]
-        + [pltpu.SemaphoreType.DMA((n,)) for n in (8, 5, 5, 13, 13)],
+        + [pltpu.SemaphoreType.DMA((n,)) for n in (8, 4, 4, 13, 13)],
         compiler_params=pltpu.CompilerParams(
             collective_id=0, has_side_effects=True, vmem_limit_bytes=VMEM_LIMIT
         ),

time: 46.9 us -> 48.1 us (1.026)
  Pallas kernels: 46.1 us -> 47.3 us
    pallas_call x1, Pallas kernels: 44 us -> 45.2 us  [collide_all(): pl.pallas_call(main_kernel, out_shape=[pltpu.VMEM(s, f32) for s in shapes...]
where the time goes in v7:
time: 48.1 us; the launch traced here: 48 us
  Pallas kernels  47.3 us (98%)
  between operations  0.64 us (1%)
    pallas_call x1, Pallas kernels, collide_all(): pl.pallas_call(main_kernel, out_shape=[pltpu.VMEM(s, f32) for s in shapes...  45.2 us
    pallas_call x1, Pallas kernels, store_all(): pl.pallas_call(store_kernel, out_shape=[jax.ShapeDtypeStruct(s, f32) for...  2.15 us

profile of v7, /device:TPU:1, one launch (start us, length us, event | category | flops | bytes accessed | tf_op | source)
XLA Modules:
  0.0 48.0 jit_solution(16137547463287525159)
XLA Ops:
  0.6 45.2 %collision.1 = (f32[33,256,128]{2,1,0:T(8,128)S(1)}, f32[256,128]{1,0:T(8,128)S(1)}) custom-call(f32[16]{0:T(128)} %table_ref.1, f32[7,256,128]{2,1,0:T(8,128)} %bitcast.9, f32[7,256,128]{2,1,0:T(8,128)} %bitcast.10, f32[19,256,128]{2,1,0:T(8,128)} %bitcast.8, s32[256,128]{1,0:T(8,128)} %bitcast.11, f32[128,256]{1,0:T(8,128)} %constant.8.clone.hy_hbm, ...), custom_call_target="tpu_custom_call" | custom-call | tf_op jit(solution)/shard_map/collision/pallas_call | solution.py:817
  45.8 2.2 %results.1 = (f32[19,256,128]{2,1,0:T(8,128)}, f32[7,256,128]{2,1,0:T(8,128)}, f32[7,256,128]{2,1,0:T(8,128)}, f32[256,128]{1,0:T(8,128)}) custom-call(f32[33,256,128]{2,1,0:T(8,128)S(1)} %get-tuple-element.10.moved, f32[256,128]{1,0:T(8,128)S(1)} %get-tuple-element.11.phi), custom_call_target="tpu_custom_call" | custom-call | tf_op jit(solution)/shard_map/results/pallas_call | solution.py:848
